TPU v7x, 32 devices: a whole 2x2x4 slice. The times are simulated.
32 devices in a mesh: gx: 8 (over z, y), gy: 4 (over x, core).
Axes of the slice: x: 2, y: 2, z: 4, core: 2. Of those that a mesh axis runs over, the one named last changes fastest.
Arguments:
- vectors: float32 [8, 3, 4, 64, 512], P(None, None, None, 'gx', 'gy'), may hold values from -2000 to 2000, as said below
- background: float32 [3, 4, 64, 512], P(None, None, 'gx', 'gy'), may hold values from -1 to 1
- obs_site: int32 [131072], P(('gx', 'gy')), may hold values from 0 to 12287
- obs_offset: float32 [2, 131072], P(None, ('gx', 'gy')), may hold values from -1 to 1
- obs_error: float32 [131072], P(('gx', 'gy')), may hold values from 0.5 to 4
Outputs:
- analysis: float32 [8, 3, 4, 64, 512], P(None, None, None, 'gx', 'gy')
- obs_perturb: float32 [8, 131072], P(None, ('gx', 'gy'))
Inputs may be any that keep to these rules, and one draw needn't show every extreme that they name: Drawn with scales that vary over vectors, variables, levels and cells. `obs_site`: observation n lies in the tile of device n // 4096; its site is ((variable * 4 + level) * 8 + row) * 128 + column, with row and column local to that tile.
All inputs are finite; a program needn't handle non-finite values.
Results may differ from a plain program's by a relative error of at most 0.000092.
Values sent between devices are 32-bit elements; how exact they have to be, the bound alone decides.
A program may use at most 192 MiB of HBM per device.

v0:
```python
import jax
import jax.numpy as jnp
from jax import lax
from jax.sharding import PartitionSpec as P

L = 4


step_size = 0.35
highest = lax.Precision.HIGHEST


def padded_2(block, sides, width):
    for axis, dim in sides:
        count = lax.axis_size(axis)
        forward = [(i, i + 1) for i in range(count - 1)]
        forward.append((count - 1, 0))
        backward = [(target, source) for source, target in forward]
        low = lax.ppermute(
            lax.slice_in_dim(block, block.shape[dim] - width, None, axis=dim), axis, forward
        )
        high = lax.ppermute(lax.slice_in_dim(block, 0, width, axis=dim), axis, backward)
        block = jnp.concatenate([low, block, high], axis=dim)
    return block


def trim_rim(field, width):
    return field[..., width : field.shape[-2] - width, width : field.shape[-1] - width]


def tendency(padded, background):

    def along_x(field):
        return 0.5 * (field[..., 2:, 1:-1] - field[..., :-2, 1:-1])

    def along_y(field):
        return 0.5 * (field[..., 1:-1, 2:] - field[..., 1:-1, :-2])

    wind_x, wind_y, vort_abs = (background[0], background[1], background[2])
    east_part = padded[:, 0]
    north_part = padded[:, 1]
    height = padded[:, 2]

    def advect(field):
        return wind_x * along_x(field) + wind_y * along_y(field)

    tend_east = -advect(east_part) - along_x(height) + vort_abs * trim_rim(north_part, 1)
    tend_north = -advect(north_part) - along_y(height) - vort_abs * trim_rim(east_part, 1)
    tend_height = -advect(height) - (along_x(east_part) + along_y(north_part))
    return jnp.stack([tend_east, tend_north, tend_height], axis=1)


def section_rims(field):
    return padded_2(field, (("gx", 3), ("gy", 4)), 1)


def final_rims(field):
    return padded_2(field, (("gx", 3), ("gy", 4)), 1)


def sample(rimmed, obs_site, obs_offset):
    vector_count = rimmed.shape[0]
    rows_dev = rimmed.shape[3] - 2
    cols_dev = rimmed.shape[4] - 2
    windows = []
    for step_x in (-1, 0, 1):
        for step_y in (-1, 0, 1):
            window = rimmed[
                :, :, :, 1 + step_x : 1 + step_x + rows_dev, 1 + step_y : 1 + step_y + cols_dev
            ]
            windows.append(window.reshape(vector_count, -1))
    table = jnp.concatenate(windows, axis=0).T
    picked = jnp.take(table, obs_site, axis=0).reshape(obs_site.shape[0], 9, vector_count)
    shift_x = obs_offset[0]
    shift_y = obs_offset[1]
    weights_x = (jnp.maximum(-shift_x, 0.0), 1.0 - jnp.abs(shift_x), jnp.maximum(shift_x, 0.0))
    weights_y = (jnp.maximum(-shift_y, 0.0), 1.0 - jnp.abs(shift_y), jnp.maximum(shift_y, 0.0))
    pair_weights = jnp.stack(
        [weights_x[i] * weights_y[j] for i in range(3) for j in range(3)], axis=1
    )
    return jnp.einsum(
        "ow,owk->ko", pair_weights, picked, precision=highest, preferred_element_type=jnp.float32
    )


def local(vectors, background, obs_site, obs_offset, obs_error):
    vector_count = vectors.shape[0]
    devices_all = lax.axis_size("gx") * lax.axis_size("gy")
    cells_all = float(3 * L * vectors.shape[3] * vectors.shape[4] * devices_all)
    obs_all = float(obs_site.shape[0] * devices_all)
    identity = jnp.eye(vector_count, dtype=jnp.float32)
    section_one = vectors + step_size * tendency(section_rims(vectors), background)
    section_two = 0.75 * vectors + 0.25 * (
        section_one + step_size * tendency(section_rims(section_one), background)
    )
    bred = vectors / 3.0 + 2.0 / 3.0 * (
        section_two + step_size * tendency(section_rims(section_two), background)
    )
    flattened = bred.reshape(vector_count, -1)
    gram_local = jnp.dot(
        flattened, flattened.T, precision=highest, preferred_element_type=jnp.float32
    )
    gram = lax.psum(gram_local, ("gx", "gy")) / cells_all
    lower = jnp.linalg.cholesky(gram)
    inv_lower = lax.linalg.triangular_solve(lower, identity, left_side=True, lower=True)
    basis = jnp.dot(inv_lower, flattened, precision=highest, preferred_element_type=jnp.float32)
    basis_rim = final_rims(basis.reshape(bred.shape))
    projected = sample(basis_rim, obs_site, obs_offset)
    normal_local = jnp.dot(
        projected / obs_error, projected.T, precision=highest, preferred_element_type=jnp.float32
    )
    normal = lax.psum(normal_local, ("gx", "gy")) / obs_all
    factor = jnp.linalg.cholesky(identity + normal)
    combo = lax.linalg.triangular_solve(factor, identity, left_side=True, lower=True)
    analysis = jnp.dot(combo, basis, precision=highest, preferred_element_type=jnp.float32).reshape(
        bred.shape
    )
    obs_perturb = jnp.dot(
        combo, projected, precision=highest, preferred_element_type=jnp.float32
    ) / jnp.sqrt(obs_error)
    return (analysis, obs_perturb)


def solution(mesh):
    placed = (
        P(None, None, None, "gx", "gy"),
        P(None, None, "gx", "gy"),
        P(("gx", "gy")),
        P(None, ("gx", "gy")),
        P(("gx", "gy")),
    )
    return jax.shard_map(
        local,
        mesh=mesh,
        in_specs=placed,
        out_specs=(P(None, None, None, "gx", "gy"), P(None, ("gx", "gy"))),
        check_vma=False,
    )
```

profile of v0, /device:TPU:0, one launch (start us, length us, event | category | flops | bytes accessed | tf_op | source)
XLA Modules:
  0.0 212.1 jit_solution(14498992246684601436)
XLA Ops:
  1.8 3.0 %collective-permute-start = (f32[8,3,4,1,128]{4,0,3,2,1:T(8,128)S(1)}, f32[8,3,4,1,128]{4,0,3,2,1:T(8,128)S(1)}, u32[]{:S(2)}, u32[]{:S(2)}) collective-permute-start(f32[8,3,4,1,128]{4,0,3,2,1:T(8,128)S(1)} %copy.182), channel_id=1, source_target_pairs={{0,4},{4,8},{8,12},{12,16},{16,20},{20,24},{24,28},{28,0},{1,5},{5... | collective-permute-start | bytes 147464 | tf_op jit(solution)/shard_map/ppermute | solution.py:19
  4.9 3.1 %collective-permute-start.1 = (f32[8,3,4,1,128]{4,0,3,2,1:T(8,128)S(1)}, f32[8,3,4,1,128]{4,0,3,2,1:T(8,128)S(1)}, u32[]{:S(2)}, u32[]{:S(2)}) collective-permute-start(f32[8,3,4,1,128]{4,0,3,2,1:T(8,128)S(1)} %copy.181), channel_id=1, source_target_pairs={{4,0},{8,4},{12,8},{16,12},{20,16},{24,20},{28,24},{0,28},{5,1},{9... | collective-permute-start | bytes 147464 | tf_op jit(solution)/shard_map/ppermute | solution.py:22
  8.0 4.8 %copy.141 = f32[8,3,4,8,128]{3,0,4,2,1:T(8,128)} copy(f32[8,3,4,8,128]{4,3,2,1,0:T(8,128)} %param.8) | data formatting | bytes 786432 | tf_op args[0]
  12.8 4.0 %copy.140 = f32[8,3,4,1,128]{3,0,4,2,1:T(8,128)} copy(f32[8,3,4,1,128]{4,0,3,2,1:T(8,128)S(1)} %collective-permute-done) | data formatting | bytes 98304 | tf_op jit(solution)/shard_map/ppermute | solution.py:19
  16.8 4.0 %copy.142 = f32[8,3,4,1,128]{3,0,4,2,1:T(8,128)} copy(f32[8,3,4,1,128]{4,0,3,2,1:T(8,128)S(1)} %collective-permute-done.1) | data formatting | bytes 98304 | tf_op jit(solution)/shard_map/ppermute | solution.py:22
  20.8 8.2 %pad_maximum_fusion = f32[8,3,4,10,128]{3,0,4,2,1:T(8,128)S(1)} fusion(f32[8,3,4,1,128]{3,0,4,2,1:T(8,128)} %copy.142, f32[8,3,4,8,128]{3,0,4,2,1:T(8,128)} %copy.141, f32[8,3,4,1,128]{3,0,4,2,1:T(8,128)} %copy.140), kind=kLoop, calls=%fused_computation.1 | loop fusion | flops 245760 | bytes 983040 | tf_op jit(solution)/shard_map/concatenate | solution.py:23
  28.9 2.7 %copy-done = f32[8,3,4,10,128]{3,0,4,2,1:T(8,128)} copy-done((f32[8,3,4,10,128]{3,0,4,2,1:T(8,128)}, f32[8,3,4,10,128]{3,0,4,2,1:T(8,128)S(1)}, u32[]{:S(2)}) %copy-start) | copy-done | bytes 491544
  31.7 1.7 collective-permute-start.3
  33.4 4.5 %copy.144 = f32[8,3,4,10,128]{4,0,3,2,1:T(8,128)S(1)} copy(f32[8,3,4,10,128]{3,0,4,2,1:T(8,128)} %copy-done) | data formatting | bytes 983040 | tf_op jit(solution)/shard_map/concatenate | solution.py:23
  40.9 4.7 %collective-permute-start.5 = (f32[8,3,4,1,128]{4,0,3,2,1:T(8,128)S(1)}, f32[8,3,4,1,128]{4,0,3,2,1:T(8,128)S(1)}, u32[]{:S(2)}, u32[]{:S(2)}) collective-permute-start(f32[8,3,4,1,128]{4,0,3,2,1:T(8,128)S(1)} %get-tuple-element.54), channel_id=1, source_target_pairs={{4,0},{8,4},{12,8},{16,12},{20,16},{24,20},{28,24},{0,28},{5,1},{9... | collective-permute-start | bytes 147464 | tf_op jit(solution)/shard_map/ppermute | solution.py:22
  45.6 2.1 collective-permute-done.4
  49.3 1.8 collective-permute-start.7
  55.1 4.8 %collective-permute-start.9 = (f32[8,3,4,1,128]{4,0,3,2,1:T(8,128)S(1)}, f32[8,3,4,1,128]{4,0,3,2,1:T(8,128)S(1)}, u32[]{:S(2)}, u32[]{:S(2)}) collective-permute-start(f32[8,3,4,1,128]{4,0,3,2,1:T(8,128)S(1)} %get-tuple-element.52), channel_id=1, source_target_pairs={{4,0},{8,4},{12,8},{16,12},{20,16},{24,20},{28,24},{0,28},{5,1},{9... | collective-permute-start | bytes 147464 | tf_op jit(solution)/shard_map/ppermute | solution.py:22
  60.0 1.9 collective-permute-done.8
  70.5 40.5 %psum.14 = f32[8,8]{0,1:T(8,128)S(1)} all-reduce(f32[8,8]{0,1:T(8,128)S(1)} %convolution_bitcast_fusion), channel_id=1, replica_groups=mesh['gx'=8,'gy'=4] {'gx','gy'}, use_global_device_ids=true, to_apply=%region_0.0 | all-reduce | flops 64 | bytes 512 | tf_op jit(solution)/shard_map/psum | solution.py:103
  114.4 2.3 %collective-permute-start.12 = (f32[8,3,4,1,128]{4,0,3,2,1:T(8,128)S(1)}, f32[8,3,4,1,128]{4,0,3,2,1:T(8,128)S(1)}, u32[]{:S(2)}, u32[]{:S(2)}) collective-permute-start(f32[8,3,4,1,128]{4,0,3,2,1:T(8,128)S(1)} %get-tuple-element.49), channel_id=1, source_target_pairs={{0,4},{4,8},{8,12},{12,16},{16,20},{20,24},{24,28},{28,0},{1,5},{5... | collective-permute-start | bytes 147464 | tf_op jit(solution)/shard_map/ppermute | solution.py:19
  116.7 2.5 %collective-permute-start.13 = (f32[8,3,4,1,128]{4,0,3,2,1:T(8,128)S(1)}, f32[8,3,4,1,128]{4,0,3,2,1:T(8,128)S(1)}, u32[]{:S(2)}, u32[]{:S(2)}) collective-permute-start(f32[8,3,4,1,128]{4,0,3,2,1:T(8,128)S(1)} %get-tuple-element.50), channel_id=1, source_target_pairs={{4,0},{8,4},{12,8},{16,12},{20,16},{24,20},{28,24},{0,28},{5,1},{9... | collective-permute-start | bytes 147464 | tf_op jit(solution)/shard_map/ppermute | solution.py:22
  119.5 1.9 collective-permute-done.12
  121.6 1.7 collective-permute-start.15
  123.4 9.2 %collective-permute-done.14 = f32[8,3,4,10,1]{4,0,3,2,1:T(8,128)S(1)} collective-permute-done((f32[8,3,4,10,1]{4,0,3,2,1:T(8,128)S(1)}, f32[8,3,4,10,1]{4,0,3,2,1:T(8,128)S(1)}, u32[]{:S(2)}, u32[]{:S(2)}) %collective-permute-start.14) | collective-permute-done | bytes 3872 | tf_op jit(solution)/shard_map/ppermute | solution.py:19
  132.6 2.2 %collective-permute-done.15 = f32[8,3,4,10,1]{4,0,3,2,1:T(8,128)S(1)} collective-permute-done((f32[8,3,4,10,1]{4,0,3,2,1:T(8,128)S(1)}, f32[8,3,4,10,1]{4,0,3,2,1:T(8,128)S(1)}, u32[]{:S(2)}, u32[]{:S(2)}) %collective-permute-start.15) | collective-permute-done | bytes 3872 | tf_op jit(solution)/shard_map/ppermute | solution.py:22
  142.7 5.9 %copy.158 = f32[12288,72]{1,0:T(8,128)} copy(f32[12288,72]{0,1:T(8,128)} %bitcast.35) | data formatting | bytes 7077888 | tf_op jit(solution)/shard_map/transpose | solution.py:72
  148.6 13.6 %gather_fusion = f32[4096,72]{1,0:T(8,128)S(1)} fusion(f32[12288,72]{1,0:T(8,128)} %copy.158, s32[4096]{0:T(1024)S(1)} %fusion.48), kind=kCustom, calls=%fused_computation | custom fusion | bytes 2375680 | tf_op jit(solution)/shard_map/jit(_take)/gather | solution.py:73
  165.6 41.3 %psum.15 = f32[8,8]{0,1:T(8,128)S(1)} all-reduce(f32[8,8]{0,1:T(8,128)S(1)} %fusion.9), channel_id=1, replica_groups=mesh['gx'=8,'gy'=4] {'gx','gy'}, use_global_device_ids=true, to_apply=%region_3.6 | all-reduce | flops 64 | bytes 512 | tf_op jit(solution)/shard_map/psum | solution.py:112
  (111 shorter events, 38.9 us)
Async XLA Ops:
  1.8 11.0 %collective-permute-start = (f32[8,3,4,1,128]{4,0,3,2,1:T(8,128)S(1)}, f32[8,3,4,1,128]{4,0,3,2,1:T(8,128)S(1)}, u32[]{:S(2)}, u32[]{:S(2)}) collective-permute-start(f32[8,3,4,1,128]{4,0,3,2,1:T(8,128)S(1)} %copy.182), channel_id=1, source_target_pairs={{0,4},{4,8},{8,12},{12,16},{16,20},{20,24},{24,28},{28,0},{1,5},{5... | collective-permute-start | bytes 147464 | tf_op jit(solution)/shard_map/ppermute | solution.py:19
  4.9 11.9 %collective-permute-start.1 = (f32[8,3,4,1,128]{4,0,3,2,1:T(8,128)S(1)}, f32[8,3,4,1,128]{4,0,3,2,1:T(8,128)S(1)}, u32[]{:S(2)}, u32[]{:S(2)}) collective-permute-start(f32[8,3,4,1,128]{4,0,3,2,1:T(8,128)S(1)} %copy.181), channel_id=1, source_target_pairs={{4,0},{8,4},{12,8},{16,12},{20,16},{24,20},{28,24},{0,28},{5,1},{9... | collective-permute-start | bytes 147464 | tf_op jit(solution)/shard_map/ppermute | solution.py:22
  20.8 12.6 %copy-start.3 = (f32[3,4,8,128]{3,2,1,0:T(8,128)S(1)}, f32[3,4,8,128]{3,2,1,0:T(8,128)}, u32[]{:S(2)}) copy-start(f32[3,4,8,128]{3,2,1,0:T(8,128)} %param.9) | copy-start | bytes 147460
  28.9 2.7 %copy-start = (f32[8,3,4,10,128]{3,0,4,2,1:T(8,128)}, f32[8,3,4,10,128]{3,0,4,2,1:T(8,128)S(1)}, u32[]{:S(2)}) copy-start(f32[8,3,4,10,128]{3,0,4,2,1:T(8,128)S(1)} %pad_maximum_fusion) | copy-start | bytes 1474564
  31.6 6.3 %collective-permute-start.2 = (f32[8,3,4,10,1]{3,0,4,2,1:T(8,128)S(1)}, f32[8,3,4,10,1]{3,0,4,2,1:T(8,128)S(1)}, u32[]{:S(2)}, u32[]{:S(2)}) collective-permute-start(f32[8,3,4,10,1]{3,0,4,2,1:T(8,128)S(1)} %get-tuple-element.16), channel_id=1, source_target_pairs={{0,1},{1,2},{2,3},{3,0},{4,5},{5,6},{6,7},{7,4},{8,9},{9,10},{10,1... | collective-permute-start | bytes 11528 | tf_op jit(solution)/shard_map/ppermute | solution.py:19
  31.7 6.9 %collective-permute-start.3 = (f32[8,3,4,10,1]{3,0,4,2,1:T(8,128)S(1)}, f32[8,3,4,10,1]{3,0,4,2,1:T(8,128)S(1)}, u32[]{:S(2)}, u32[]{:S(2)}) collective-permute-start(f32[8,3,4,10,1]{3,0,4,2,1:T(8,128)S(1)} %get-tuple-element.17), channel_id=1, source_target_pairs={{1,0},{2,1},{3,2},{0,3},{5,4},{6,5},{7,6},{4,7},{9,8},{10,9},{11,1... | collective-permute-start | bytes 11528 | tf_op jit(solution)/shard_map/ppermute | solution.py:22
  39.2 1.3 copy-start.1
  40.8 6.8 %collective-permute-start.4 = (f32[8,3,4,1,128]{4,0,3,2,1:T(8,128)S(1)}, f32[8,3,4,1,128]{4,0,3,2,1:T(8,128)S(1)}, u32[]{:S(2)}, u32[]{:S(2)}) collective-permute-start(f32[8,3,4,1,128]{4,0,3,2,1:T(8,128)S(1)} %get-tuple-element.53), channel_id=1, source_target_pairs={{0,4},{4,8},{8,12},{12,16},{16,20},{20,24},{24,28},{28,0},{1,5},{5... | collective-permute-start | bytes 147464 | tf_op jit(solution)/shard_map/ppermute | solution.py:19
  40.9 6.8 %collective-permute-start.5 = (f32[8,3,4,1,128]{4,0,3,2,1:T(8,128)S(1)}, f32[8,3,4,1,128]{4,0,3,2,1:T(8,128)S(1)}, u32[]{:S(2)}, u32[]{:S(2)}) collective-permute-start(f32[8,3,4,1,128]{4,0,3,2,1:T(8,128)S(1)} %get-tuple-element.54), channel_id=1, source_target_pairs={{4,0},{8,4},{12,8},{16,12},{20,16},{24,20},{28,24},{0,28},{5,1},{9... | collective-permute-start | bytes 147464 | tf_op jit(solution)/shard_map/ppermute | solution.py:22
  48.5 3.5 %collective-permute-start.6 = (f32[8,3,4,10,1]{3,0,4,2,1:T(8,128)S(1)}, f32[8,3,4,10,1]{3,0,4,2,1:T(8,128)S(1)}, u32[]{:S(2)}, u32[]{:S(2)}) collective-permute-start(f32[8,3,4,10,1]{3,0,4,2,1:T(8,128)S(1)} %copy.171), channel_id=1, source_target_pairs={{0,1},{1,2},{2,3},{3,0},{4,5},{5,6},{6,7},{7,4},{8,9},{9,10},{10,1... | collective-permute-start | bytes 11528 | tf_op jit(solution)/shard_map/ppermute | solution.py:19
  49.3 3.5 %collective-permute-start.7 = (f32[8,3,4,10,1]{3,0,4,2,1:T(8,128)S(1)}, f32[8,3,4,10,1]{3,0,4,2,1:T(8,128)S(1)}, u32[]{:S(2)}, u32[]{:S(2)}) collective-permute-start(f32[8,3,4,10,1]{3,0,4,2,1:T(8,128)S(1)} %copy.172), channel_id=1, source_target_pairs={{1,0},{2,1},{3,2},{0,3},{5,4},{6,5},{7,6},{4,7},{9,8},{10,9},{11,1... | collective-permute-start | bytes 11528 | tf_op jit(solution)/shard_map/ppermute | solution.py:22
  53.9 6.0 %copy-start.4 = (f32[2,4096]{1,0:T(2,128)S(1)}, f32[2,4096]{1,0:T(2,128)}, u32[]{:S(2)}) copy-start(f32[2,4096]{1,0:T(2,128)} %param.11) | copy-start | bytes 98308
  54.4 11.0 %copy-start.2 = (s32[4096]{0:T(1024)S(1)}, s32[4096]{0:T(1024)}, u32[]{:S(2)}) copy-start(s32[4096]{0:T(1024)} %param.10) | copy-start | bytes 49156
  55.1 6.8 %collective-permute-start.8 = (f32[8,3,4,1,128]{4,0,3,2,1:T(8,128)S(1)}, f32[8,3,4,1,128]{4,0,3,2,1:T(8,128)S(1)}, u32[]{:S(2)}, u32[]{:S(2)}) collective-permute-start(f32[8,3,4,1,128]{4,0,3,2,1:T(8,128)S(1)} %get-tuple-element.51), channel_id=1, source_target_pairs={{0,4},{4,8},{8,12},{12,16},{16,20},{20,24},{24,28},{28,0},{1,5},{5... | collective-permute-start | bytes 147464 | tf_op jit(solution)/shard_map/ppermute | solution.py:19
  55.1 6.8 %collective-permute-start.9 = (f32[8,3,4,1,128]{4,0,3,2,1:T(8,128)S(1)}, f32[8,3,4,1,128]{4,0,3,2,1:T(8,128)S(1)}, u32[]{:S(2)}, u32[]{:S(2)}) collective-permute-start(f32[8,3,4,1,128]{4,0,3,2,1:T(8,128)S(1)} %get-tuple-element.52), channel_id=1, source_target_pairs={{4,0},{8,4},{12,8},{16,12},{20,16},{24,20},{28,24},{0,28},{5,1},{9... | collective-permute-start | bytes 147464 | tf_op jit(solution)/shard_map/ppermute | solution.py:22
  62.8 3.5 %collective-permute-start.10 = (f32[8,3,4,10,1]{3,0,4,2,1:T(8,128)S(1)}, f32[8,3,4,10,1]{3,0,4,2,1:T(8,128)S(1)}, u32[]{:S(2)}, u32[]{:S(2)}) collective-permute-start(f32[8,3,4,10,1]{3,0,4,2,1:T(8,128)S(1)} %copy.173), channel_id=1, source_target_pairs={{0,1},{1,2},{2,3},{3,0},{4,5},{5,6},{6,7},{7,4},{8,9},{9,10},{10,1... | collective-permute-start | bytes 11528 | tf_op jit(solution)/shard_map/ppermute | solution.py:19
  64.3 2.9 %collective-permute-start.11 = (f32[8,3,4,10,1]{3,0,4,2,1:T(8,128)S(1)}, f32[8,3,4,10,1]{3,0,4,2,1:T(8,128)S(1)}, u32[]{:S(2)}, u32[]{:S(2)}) collective-permute-start(f32[8,3,4,10,1]{3,0,4,2,1:T(8,128)S(1)} %copy.174), channel_id=1, source_target_pairs={{1,0},{2,1},{3,2},{0,3},{5,4},{6,5},{7,6},{4,7},{9,8},{10,9},{11,1... | collective-permute-start | bytes 11528 | tf_op jit(solution)/shard_map/ppermute | solution.py:22
  68.4 50.8 %copy-start.5 = (f32[4096]{0:T(1024)S(1)}, f32[4096]{0:T(1024)}, u32[]{:S(2)}) copy-start(f32[4096]{0:T(1024)} %param.12) | copy-start | bytes 49156
  114.4 6.9 %collective-permute-start.12 = (f32[8,3,4,1,128]{4,0,3,2,1:T(8,128)S(1)}, f32[8,3,4,1,128]{4,0,3,2,1:T(8,128)S(1)}, u32[]{:S(2)}, u32[]{:S(2)}) collective-permute-start(f32[8,3,4,1,128]{4,0,3,2,1:T(8,128)S(1)} %get-tuple-element.49), channel_id=1, source_target_pairs={{0,4},{4,8},{8,12},{12,16},{16,20},{20,24},{24,28},{28,0},{1,5},{5... | collective-permute-start | bytes 147464 | tf_op jit(solution)/shard_map/ppermute | solution.py:19
  116.7 4.6 %collective-permute-start.13 = (f32[8,3,4,1,128]{4,0,3,2,1:T(8,128)S(1)}, f32[8,3,4,1,128]{4,0,3,2,1:T(8,128)S(1)}, u32[]{:S(2)}, u32[]{:S(2)}) collective-permute-start(f32[8,3,4,1,128]{4,0,3,2,1:T(8,128)S(1)} %get-tuple-element.50), channel_id=1, source_target_pairs={{4,0},{8,4},{12,8},{16,12},{20,16},{24,20},{28,24},{0,28},{5,1},{9... | collective-permute-start | bytes 147464 | tf_op jit(solution)/shard_map/ppermute | solution.py:22
  121.6 11.0 %collective-permute-start.14 = (f32[8,3,4,10,1]{4,0,3,2,1:T(8,128)S(1)}, f32[8,3,4,10,1]{4,0,3,2,1:T(8,128)S(1)}, u32[]{:S(2)}, u32[]{:S(2)}) collective-permute-start(f32[8,3,4,10,1]{4,0,3,2,1:T(8,128)S(1)} %get-tuple-element.42), channel_id=1, source_target_pairs={{0,1},{1,2},{2,3},{3,0},{4,5},{5,6},{6,7},{7,4},{8,9},{9,10},{10,1... | collective-permute-start | bytes 11528 | tf_op jit(solution)/shard_map/ppermute | solution.py:19
  121.6 13.2 %collective-permute-start.15 = (f32[8,3,4,10,1]{4,0,3,2,1:T(8,128)S(1)}, f32[8,3,4,10,1]{4,0,3,2,1:T(8,128)S(1)}, u32[]{:S(2)}, u32[]{:S(2)}) collective-permute-start(f32[8,3,4,10,1]{4,0,3,2,1:T(8,128)S(1)} %get-tuple-element.41), channel_id=1, source_target_pairs={{1,0},{2,1},{3,2},{0,3},{5,4},{6,5},{7,6},{4,7},{9,8},{10,9},{11,1... | collective-permute-start | bytes 11528 | tf_op jit(solution)/shard_map/ppermute | solution.py:22
where the time goes:
time: 213 us; the launch traced here: 212 us
  blocking collectives  81.8 us (38%)
  local copies, waits for them, and re-layouts  58.5 us (27%)
  starting transfers between devices  27.8 us (13%)
  other arithmetic  20 us (9%)
  waiting for transfers between devices  19.4 us (9%)
  matrix products  3.54 us (2%)
    psum x1, blocking collectives, local(): normal = lax.psum(normal_local, ('gx', 'gy')) / obs_all  41.3 us
    psum x1, blocking collectives, local(): gram = lax.psum(gram_local, ('gx', 'gy')) / cells_all  40.5 us
    ppermute x8, starting transfers between devices, padded_2(): lax.ppermute(lax.slice_in_dim(block, 0, width, axis=dim), axis, backward)  21.4 us
    unnamed x28, local copies, waits for them, and re-layouts  17.4 us
    ppermute x8, waiting for transfers between devices, padded_2(): lax.ppermute(lax.slice_in_dim(block, block.shape[dim] - width, None, axis...  17 us
    gather x2, local copies, waits for them, and re-layouts, sample(): jnp.take(table, obs_site, axis=0)  15.2 us
    concatenate x9, other arithmetic, padded_2(): block = jnp.concatenate([low, block, high], axis=dim)  10 us
    ppermute x8, starting transfers between devices, padded_2(): lax.ppermute(lax.slice_in_dim(block, block.shape[dim] - width, None, axis...  6.46 us
  transfers between devices with their start and end apart: 16, of which 8 were waited for; matrix products, arithmetic and copies ran while one was open for 8% of the time, Pallas kernels for 0%

commit v1 on v0

v1 whole, which is shorter than its diff:
```python
import functools

import jax
import jax.numpy as jnp
from jax import lax
from jax.experimental import pallas as pl
from jax.experimental.pallas import tpu as pltpu
from jax.sharding import PartitionSpec as P

K = 8
V = 3
L = 4
ROWS = 8
COLS = 128
PLANES = V * L
STRIDE = PLANES * ROWS
STEP = 0.35
MESH = pl.DeviceIdType.MESH
SHIFTS = 5
N_EDGE = 8
N_COPIES = N_EDGE + 2 + 2 * L


def increments(below, here, above, west, east, bg):
    wx, wy, va = bg
    dx = [above[i] - below[i] for i in range(V)]
    dy = [east[i] - west[i] for i in range(V)]
    half = 0.5 * STEP
    hx, hy, sv = half * wx, half * wy, STEP * va
    inc_e = sv * here[1] - (hx * dx[0] + hy * dy[0]) - half * dx[2]
    inc_n = -(sv * here[0]) - (hx * dx[1] + hy * dy[1]) - half * dy[2]
    inc_h = -(hx * dx[2] + hy * dy[2]) - half * (dx[0] + dy[1])
    return inc_e, inc_n, inc_h


def advance(stage, start, here, inc):
    if stage == 0:
        return here + inc
    if stage == 1:
        return 0.75 * start + 0.25 * (here + inc)
    return (1.0 / 3.0) * start + (2.0 / 3.0) * (here + inc)


def lane_gather(tile, index):
    return jnp.take_along_axis(tile, index, axis=1, mode="promise_in_bounds")


def kernel(
    n_gx, n_gy, cells_all, obs_all,
    vec_ref, bg_ref, site_ref, off_ref, err_ref,
    out_ref, obs_ref,
    state, one, two, bred, bgrows, strips, edges, proj, gacc, sum_y, sum_x, part,
    send_sem, recv_sem, ysend, yrecv, xsend, xrecv,
):
    groups = site_ref.shape[0]
    gx = lax.axis_index("gx")
    gy = lax.axis_index("gy")
    up, dn = lax.rem(gx + n_gx - 1, n_gx), lax.rem(gx + 1, n_gx)
    lf, rt = lax.rem(gy + n_gy - 1, n_gy), lax.rem(gy + 1, n_gy)
    x_peers = [lax.rem(gx + d, n_gx) for d in range(1, n_gx)]
    y_peers = [lax.rem(gy + d, n_gy) for d in range(1, n_gy)]
    lane = lax.broadcasted_iota(jnp.int32, (K, COLS), 1)
    sub = lax.broadcasted_iota(jnp.int32, (K, COLS), 0)
    lane8 = lane & 7

    barrier = pltpu.get_barrier_semaphore()
    greeted = [(a, b) for a in (up, dn) for b in (lf, rt)]
    greeted += [(a, gy) for a in x_peers] + [(gx, b) for b in y_peers]
    for peer in greeted:
        pl.semaphore_signal(barrier, inc=1, device_id=peer, device_id_type=MESH)

    packed = [[jnp.zeros((K, COLS), jnp.float32) for _ in range(V + 1)] for _ in range(2)]
    for l in range(L):
        for r in range(ROWS):
            h, base = r // 4, l * 32 + (r % 4) * 8
            put = (lane >> 3) == base // 8
            for v in range(V):
                tile = vec_ref[pl.ds((v * L + l) * ROWS + r, K, stride=STRIDE), :]
                state[l, v, 4 + r] = tile
                packed[h][v] = jnp.where(put, pltpu.roll(tile, (base + 4) % COLS, 1), packed[h][v])
            rows = [
                jnp.broadcast_to(bg_ref[pl.ds((v * L + l) * ROWS + r, 1), :], (K, COLS))
                for v in range(V)
            ]
            tile = jnp.where(sub == 0, rows[0], jnp.where(sub == 1, rows[1], rows[2]))
            packed[h][V] = jnp.where(put, pltpu.roll(tile, (base + 4) % COLS, 1), packed[h][V])
        for h in range(2):
            for v in range(V):
                bgrows[1 + h, l, pl.ds(v * 4, 4), :] = bg_ref[pl.ds((v * L + l) * ROWS + h * 4, 4), :]
            bgrows[1 + h, l, pl.ds(12, 4), :] = jnp.zeros((4, COLS), jnp.float32)
    for h in range(2):
        for v in range(V + 1):
            strips[1, 1 + h, v] = packed[h][v]

    pl.semaphore_wait(barrier, len(greeted))

    def remote(src, dst, index, peer):
        return pltpu.make_async_remote_copy(
            src_ref=src, dst_ref=dst, send_sem=send_sem.at[index], recv_sem=recv_sem.at[index],
            device_id=peer, device_id_type=MESH,
        )

    both = pl.ds(1, 2)
    near = [
        remote(strips.at[1, 1], strips.at[1, 3], 0, (up, gy)),
        remote(strips.at[1, 2], strips.at[1, 0], 1, (dn, gy)),
        remote(strips.at[1, 1], strips.at[2, 3], 2, (up, lf)),
        remote(strips.at[1, 1], strips.at[0, 3], 3, (up, rt)),
        remote(strips.at[1, 2], strips.at[2, 0], 4, (dn, lf)),
        remote(strips.at[1, 2], strips.at[0, 0], 5, (dn, rt)),
        remote(strips.at[1, both], strips.at[2, both], 6, (gx, lf)),
        remote(strips.at[1, both], strips.at[0, both], 7, (gx, rt)),
        remote(bgrows.at[1], bgrows.at[3], 8, (up, gy)),
        remote(bgrows.at[2], bgrows.at[0], 9, (dn, gy)),
    ]

    def level_copies(l):
        return (
            remote(state.at[l, :, pl.ds(4, 4)], state.at[l, :, pl.ds(12, 4)], 10 + 2 * l, (up, gy)),
            remote(state.at[l, :, pl.ds(8, 4)], state.at[l, :, pl.ds(0, 4)], 11 + 2 * l, (dn, gy)),
        )

    for copy in near:
        copy.start()
    for l in range(L):
        for copy in level_copies(l):
            copy.start()

    gacc[...] = jnp.zeros_like(gacc)
    proj[...] = jnp.zeros_like(proj)
    for copy in near:
        copy.wait_recv()

    def level(l, carry):
        whole = []
        for side in range(3):
            fields = []
            for v in range(V + 1):
                tile = jnp.zeros((K, COLS), jnp.float32)
                for seg in range(4):
                    moved = pltpu.roll(strips[side, seg, v], lax.rem((seg + 4 - l) * 32, COLS), 1)
                    tile = jnp.where((lane >> 5) == seg, moved, tile)
                fields.append(tile)
            whole.append(fields)
        inner = lane8 < 4
        sides = []
        for a, b in ((0, 1), (1, 2)):
            fields = [jnp.where(inner, whole[a][v], whole[b][v]) for v in range(V + 1)]
            bg = [jnp.broadcast_to(fields[V][i : i + 1, :], (K, COLS)) for i in range(3)]
            start = fields[:V]
            here = start
            history = [start]
            for stage in range(3):
                inc = increments(
                    [pltpu.roll(f, 8, 1) for f in here], here,
                    [pltpu.roll(f, COLS - 8, 1) for f in here],
                    [pltpu.roll(f, 1, 1) for f in here],
                    [pltpu.roll(f, COLS - 1, 1) for f in here], bg,
                )
                here = [advance(stage, start[v], here[v], inc[v]) for v in range(V)]
                history.append(here)
            sides.append(history)
        for stage in range(4):
            for v in range(V):
                left, right = sides[0][stage][v], sides[1][stage][v]
                edges[stage, v] = jnp.where(
                    lane8 == 4, pltpu.roll(left, 1, 1), pltpu.roll(right, COLS - 1, 1)
                )

        for copy in level_copies(l):
            copy.wait_recv()

        def read(stage, v, q):
            if stage == 0:
                return state[l, v, q]
            return (one, two)[stage - 1][v, q]

        for stage in range(3):
            edge = [edges[stage, v] for v in range(V)]
            for q in range(1 + stage, 15 - stage):
                bg = [
                    jnp.broadcast_to(bgrows[q // 4, l, pl.ds(v * 4 + q % 4, 1), :], (K, COLS))
                    for v in range(V)
                ]
                here = [read(stage, v, q) for v in range(V)]
                rim = [pltpu.roll(edge[v], (124 - 8 * q) % COLS, 1) for v in range(V)]
                west = [jnp.where(lane == 0, rim[v], pltpu.roll(here[v], 1, 1)) for v in range(V)]
                east = [
                    jnp.where(lane == COLS - 1, rim[v], pltpu.roll(here[v], COLS - 1, 1))
                    for v in range(V)
                ]
                inc = increments(
                    [read(stage, v, q - 1) for v in range(V)], here,
                    [read(stage, v, q + 1) for v in range(V)], west, east, bg,
                )
                for v in range(V):
                    value = advance(stage, state[l, v, q], here[v], inc[v])
                    if stage == 0:
                        one[v, q] = value
                    elif stage == 1:
                        two[v, q] = value
                    else:
                        bred[l, v, q - 3] = value

        sums = [gacc[s] for s in range(SHIFTS)]
        for v in range(V):
            for rr in range(1, 9):
                tile = bred[l, v, rr]
                for s in range(SHIFTS):
                    other = tile if s == 0 else pltpu.roll(tile, K - s, 0)
                    sums[s] = sums[s] + tile * other
        for s in range(SHIFTS):
            gacc[s] = sums[s]

        def group(g, carry):
            columns = pl.ds(pl.multiple_of(g * COLS, COLS), COLS)
            site = jnp.broadcast_to(site_ref[pl.ds(g, 1), :], (K, COLS))
            a = jnp.broadcast_to(off_ref[0:1, columns], (K, COLS))
            b = jnp.broadcast_to(off_ref[1:2, columns], (K, COLS))
            plane, row, col = site >> 10, (site >> 7) & 7, site & 127
            abs_a, abs_b = jnp.abs(a), jnp.abs(b)
            row0 = jnp.where(a < 0.0, row - 1, row)
            col0 = jnp.where(b < 0.0, col - 1, col)
            wr0 = jnp.where(a < 0.0, abs_a, 1.0 - abs_a)
            wr1 = jnp.where(a < 0.0, 1.0 - abs_a, abs_a)
            wc0 = jnp.where(b < 0.0, abs_b, 1.0 - abs_b)
            wc1 = jnp.where(b < 0.0, 1.0 - abs_b, abs_b)
            past_left, past_right = col0 < 0, col0 >= COLS - 1
            w_edge = jnp.where(past_left, wc0, jnp.where(past_right, wc1, 0.0))
            wc0 = jnp.where(past_left, 0.0, wc0)
            wc1 = jnp.where(past_right, 0.0, wc1)
            at0, at1 = col0 & (COLS - 1), (col0 + 1) & (COLS - 1)
            at_edge = (row0 + 4) * 8 + jnp.where(past_left, 4, 3)
            key = (plane - l) * 16 + row0 + 1
            zero = jnp.zeros((K, COLS), jnp.float32)
            low, high, rim = zero, zero, zero
            for v in range(V):
                before = None
                for rr in range(10):
                    tile = bred[l, v, rr]
                    value = wc0 * lane_gather(tile, at0) + wc1 * lane_gather(tile, at1)
                    if before is not None:
                        high = jnp.where(before, value, high)
                    if rr < 9:
                        before = key == v * 64 + rr
                        low = jnp.where(before, value, low)
                edge = edges[3, v]
                value = wr0 * lane_gather(edge, at_edge) + wr1 * lane_gather(edge, at_edge + 8)
                rim = jnp.where(plane - l == v * 4, w_edge * value, rim)
            proj[g] += wr0 * low + wr1 * high + rim
            return carry

        lax.fori_loop(0, groups, group, 0)
        return carry

    lax.fori_loop(0, L, level, 0)

    def weigh(g, sums):
        columns = pl.ds(pl.multiple_of(g * COLS, COLS), COLS)
        tile = proj[g]
        scaled = tile / err_ref[0:1, columns]
        return tuple(
            sums[s] + scaled * (tile if s == 0 else pltpu.roll(tile, K - s, 0))
            for s in range(SHIFTS)
        )

    zero = jnp.zeros((K, COLS), jnp.float32)
    normal = lax.fori_loop(0, groups, weigh, (zero,) * SHIFTS)
    mine = zero
    for s in range(SHIFTS):
        total = gacc[s] * (1.0 / cells_all) + normal[s] * (1.0 / obs_all)
        mine = jnp.where(lane == s, jnp.sum(total, axis=1, keepdims=True), mine)

    def all_sum(value, slots, me, peers, device, sends, recvs):
        part[...] = value
        slots[me] = value
        copies = [
            pltpu.make_async_remote_copy(
                src_ref=part, dst_ref=slots.at[me], send_sem=sends.at[d], recv_sem=recvs.at[d],
                device_id=device(peer), device_id_type=MESH,
            )
            for d, peer in enumerate(peers)
        ]
        for copy in copies:
            copy.start()
        for copy in copies:
            copy.wait()
        total = slots[0]
        for i in range(1, len(peers) + 1):
            total = total + slots[i]
        return total

    mine = all_sum(mine, sum_y, gy, y_peers, lambda p: (gx, p), ysend, yrecv)
    mine = all_sum(mine, sum_x, gx, x_peers, lambda p: (p, gy), xsend, xrecv)

    matrix = jnp.where(lane == sub + K, 1.0, 0.0)
    for s in range(K):
        if s < SHIFTS:
            diagonal = mine[:, s : s + 1]
        else:
            diagonal = pltpu.roll(mine, K - s, 0)[:, K - s : K - s + 1]
        matrix = jnp.where((lane < K) & (((lane - sub) & 7) == s), diagonal, matrix)
    scale = jnp.ones((K, COLS), jnp.float32)
    for j in range(K):
        pivot_row = jnp.broadcast_to(matrix[j : j + 1, :], (K, COLS))
        pivot = jnp.broadcast_to(pivot_row[:, j : j + 1], (K, COLS))
        column = jnp.broadcast_to(matrix[:, j : j + 1], (K, COLS))
        scale = jnp.where(sub == j, pivot, scale)
        matrix = jnp.where(sub > j, matrix - (column / pivot) * pivot_row, matrix)
    matrix = matrix / jnp.sqrt(scale)
    combo = [jnp.broadcast_to(matrix[:, K + j : K + j + 1], (K, COLS)) for j in range(K)]

    def mix(tile):
        terms = [combo[j] * jnp.broadcast_to(tile[j : j + 1, :], (K, COLS)) for j in range(K)]
        while len(terms) > 1:
            terms = [terms[i] + terms[i + 1] for i in range(0, len(terms), 2)]
        return terms[0]

    def write(l, carry):
        for v in range(V):
            for r in range(ROWS):
                out_ref[pl.ds(v * L * ROWS + l * ROWS + r, K, stride=STRIDE), :] = mix(bred[l, v, r + 1])
        return carry

    lax.fori_loop(0, L, write, 0)

    def write_obs(g, carry):
        columns = pl.ds(pl.multiple_of(g * COLS, COLS), COLS)
        obs_ref[:, columns] = mix(proj[g]) / jnp.sqrt(err_ref[0:1, columns])
        return carry

    lax.fori_loop(0, groups, write_obs, 0)
    for copy in near:
        copy.wait_send()
    for l in range(L):
        for copy in level_copies(l):
            copy.wait_send()


def local(n_gx, n_gy, vectors, background, obs_site, obs_offset, obs_error):
    obs_dev = obs_site.shape[0]
    groups = obs_dev // COLS
    devices = n_gx * n_gy
    body = functools.partial(
        kernel, n_gx, n_gy, float(PLANES * ROWS * COLS * devices), float(obs_dev * devices)
    )
    f32 = jnp.float32
    vmem = pl.BlockSpec(memory_space=pltpu.VMEM)
    analysis, obs = pl.pallas_call(
        body,
        out_shape=(
            jax.ShapeDtypeStruct((K * STRIDE, COLS), f32),
            jax.ShapeDtypeStruct((K, obs_dev), f32),
        ),
        in_specs=[vmem] * 5,
        out_specs=(vmem, vmem),
        scratch_shapes=[
            pltpu.VMEM((L, V, 16, K, COLS), f32),
            pltpu.VMEM((V, 16, K, COLS), f32),
            pltpu.VMEM((V, 16, K, COLS), f32),
            pltpu.VMEM((L, V, 10, K, COLS), f32),
            pltpu.VMEM((4, L, 16, COLS), f32),
            pltpu.VMEM((3, 4, V + 1, K, COLS), f32),
            pltpu.VMEM((4, V, K, COLS), f32),
            pltpu.VMEM((groups, K, COLS), f32),
            pltpu.VMEM((SHIFTS, K, COLS), f32),
            pltpu.VMEM((n_gy, K, COLS), f32),
            pltpu.VMEM((n_gx, K, COLS), f32),
            pltpu.VMEM((K, COLS), f32),
            pltpu.SemaphoreType.DMA((N_COPIES,)),
            pltpu.SemaphoreType.DMA((N_COPIES,)),
            pltpu.SemaphoreType.DMA((n_gy - 1,)),
            pltpu.SemaphoreType.DMA((n_gy - 1,)),
            pltpu.SemaphoreType.DMA((n_gx - 1,)),
            pltpu.SemaphoreType.DMA((n_gx - 1,)),
        ],
        compiler_params=pltpu.CompilerParams(
            collective_id=0, has_side_effects=True, vmem_limit_bytes=24 * 1024 * 1024
        ),
    )(
        vectors.reshape(K * STRIDE, COLS),
        background.reshape(V * L * ROWS, COLS),
        obs_site.reshape(groups, COLS),
        obs_offset,
        obs_error.reshape(1, obs_dev),
    )
    return analysis.reshape(vectors.shape), obs


def solution(mesh):
    placed = (
        P(None, None, None, "gx", "gy"),
        P(None, None, "gx", "gy"),
        P(("gx", "gy")),
        P(None, ("gx", "gy")),
        P(("gx", "gy")),
    )
    return jax.shard_map(
        functools.partial(local, mesh.shape["gx"], mesh.shape["gy"]),
        mesh=mesh,
        in_specs=placed,
        out_specs=(P(None, None, None, "gx", "gy"), P(None, ("gx", "gy"))),
        check_vma=False,
    )
```

time: 213 us -> 63.1 us (0.30)
  blocking collectives: 81.8 us -> 0 us
  Pallas kernels: 0 us -> 56.6 us
  local copies, waits for them, and re-layouts: 58.5 us -> 5.38 us
  starting transfers between devices: 27.8 us -> 0 us
  other arithmetic: 20 us -> 0 us
  waiting for transfers between devices: 19.4 us -> 0 us
  matrix products: 3.54 us -> 0 us
    psum x2 -> x0, blocking collectives: 81.8 us -> none  [the longest x1 41.3 us: local(): normal = lax.psum(normal_local, ('gx', 'gy')) / obs_all]
    pallas_call x0 -> x1, Pallas kernels: none -> 56.6 us  [local(): pl.pallas_call(body, out_shape=(jax.ShapeDtypeStruct((K * STRIDE, COLS),...]
    ppermute x16 -> x0, starting transfers between devices: 27.8 us -> none  [the longest x8 21.4 us: padded_2(): lax.ppermute(lax.slice_in_dim(block, 0, width, axis=dim), axis, backward)]
    ppermute x16 -> x0, waiting for transfers between devices: 19.4 us -> none  [the longest x8 17 us: padded_2(): lax.ppermute(lax.slice_in_dim(block, block.shape[dim] - width, None, axis...]
    gather x2 -> x0, local copies, waits for them, and re-layouts: 15.2 us -> none  [sample(): jnp.take(table, obs_site, axis=0)]
    ppermute x8 -> x0, local copies, waits for them, and re-layouts: 12 us -> none  [the longest x4 6.02 us: padded_2(): lax.ppermute(lax.slice_in_dim(block, 0, width, axis=dim), axis, backward)]
    unnamed x28 -> x12, local copies, waits for them, and re-layouts: 17.4 us -> 5.38 us
    concatenate x9 -> x0, other arithmetic: 10 us -> none  [padded_2(): block = jnp.concatenate([low, block, high], axis=dim)]
  transfers between devices with their start and end apart: 16 -> 0, of which waited for: 8 -> 0; matrix products, arithmetic and copies ran while one was open for 8% -> 0% of each run, Pallas kernels for 0% -> 0%
where the time goes in v1:
time: 63.1 us; the launch traced here: 62.7 us
  Pallas kernels  56.6 us (90%)
  local copies, waits for them, and re-layouts  5.38 us (9%)
  between operations  0.65 us (1%)
    pallas_call x1, Pallas kernels, local(): pl.pallas_call(body, out_shape=(jax.ShapeDtypeStruct((K * STRIDE, COLS),...  56.6 us
    unnamed x12, local copies, waits for them, and re-layouts  5.38 us

profile of v1, /device:TPU:0, one launch (start us, length us, event | category | flops | bytes accessed | tf_op | source)
XLA Modules:
  0.0 62.7 jit_solution(18065625807657291679)
XLA Ops:
  0.6 0.0 copy-start
  0.6 1.0 %copy-done = f32[8,3,4,8,128]{4,3,2,1,0:T(8,128)S(1)} copy-done((f32[8,3,4,8,128]{4,3,2,1,0:T(8,128)S(1)}, f32[8,3,4,8,128]{4,3,2,1,0:T(8,128)}, u32[]{:S(2)}) %copy-start) | copy-done | bytes 393240
  1.6 0.0 copy-start.1
  1.6 0.8 %copy-done.1 = f32[3,4,8,128]{3,2,1,0:T(8,128)S(1)} copy-done((f32[3,4,8,128]{3,2,1,0:T(8,128)S(1)}, f32[3,4,8,128]{3,2,1,0:T(8,128)}, u32[]{:S(2)}) %copy-start.1) | copy-done | bytes 49176
  2.4 0.0 copy-start.2
  2.4 0.8 %copy-done.2 = f32[2,4096]{1,0:T(2,128)S(1)} copy-done((f32[2,4096]{1,0:T(2,128)S(1)}, f32[2,4096]{1,0:T(2,128)}, u32[]{:S(2)}) %copy-start.2) | copy-done | bytes 32792
  3.2 0.0 copy-start.3
  3.2 0.7 %copy-done.3 = s32[4096]{0:T(1024)S(1)} copy-done((s32[4096]{0:T(1024)S(1)}, s32[4096]{0:T(1024)}, u32[]{:S(2)}) %copy-start.3) | copy-done | bytes 16408
  3.9 0.0 copy-start.4
  3.9 0.7 %copy-done.4 = f32[4096]{0:T(1024)S(1)} copy-done((f32[4096]{0:T(1024)S(1)}, f32[4096]{0:T(1024)}, u32[]{:S(2)}) %copy-start.4) | copy-done | bytes 16408
  4.6 56.6 %shard_map.68 = (f32[768,128]{1,0:T(8,128)S(1)}, f32[8,4096]{1,0:T(8,128)S(1)}) custom-call(f32[768,128]{1,0:T(8,128)S(1)} %bitcast.6, f32[96,128]{1,0:T(8,128)S(1)} %bitcast.7, s32[32,128]{1,0:T(8,128)S(1)} %bitcast.8, f32[2,4096]{1,0:T(2,128)S(1)} %copy-done.2, f32[1,4096]{1,0:T(1,128)S(1)} %bitcast.9), custom_call_target="tpu_custom_call" | custom-call | tf_op jit(solution)/shard_map/pallas_call | solution.py:349
  61.3 0.7 %copy.9 = f32[8,3,4,8,128]{4,3,2,1,0:T(8,128)} copy(f32[8,3,4,8,128]{4,3,2,1,0:T(8,128)S(1)} %bitcast.5) | data formatting | bytes 786432
  62.0 0.7 %copy.10 = f32[8,4096]{1,0:T(8,128)} copy(f32[8,4096]{1,0:T(8,128)S(1)} %get-tuple-element.9) | data formatting | bytes 262144
Async XLA Ops:
  0.6 1.0 %copy-start = (f32[8,3,4,8,128]{4,3,2,1,0:T(8,128)S(1)}, f32[8,3,4,8,128]{4,3,2,1,0:T(8,128)}, u32[]{:S(2)}) copy-start(f32[8,3,4,8,128]{4,3,2,1,0:T(8,128)} %param.5) | copy-start | bytes 1179652
  1.6 0.8 %copy-start.1 = (f32[3,4,8,128]{3,2,1,0:T(8,128)S(1)}, f32[3,4,8,128]{3,2,1,0:T(8,128)}, u32[]{:S(2)}) copy-start(f32[3,4,8,128]{3,2,1,0:T(8,128)} %param.6) | copy-start | bytes 147460
  2.4 0.8 %copy-start.2 = (f32[2,4096]{1,0:T(2,128)S(1)}, f32[2,4096]{1,0:T(2,128)}, u32[]{:S(2)}) copy-start(f32[2,4096]{1,0:T(2,128)} %off_ref.1) | copy-start | bytes 98308
  3.2 0.7 %copy-start.3 = (s32[4096]{0:T(1024)S(1)}, s32[4096]{0:T(1024)}, u32[]{:S(2)}) copy-start(s32[4096]{0:T(1024)} %param.7) | copy-start | bytes 49156
  3.9 0.7 %copy-start.4 = (f32[4096]{0:T(1024)S(1)}, f32[4096]{0:T(1024)}, u32[]{:S(2)}) copy-start(f32[4096]{0:T(1024)} %param.9) | copy-start | bytes 49156

commit v2 on v1

--- a/solution.py
+++ b/solution.py
@@ -18,6 +18,8 @@
 MESH = pl.DeviceIdType.MESH
 SHIFTS = 5
 N_EDGE = 8
+M_ROWS = V * 10 * K
+WIDE = 512
 N_COPIES = N_EDGE + 2 + 2 * L
 
 
@@ -41,18 +43,22 @@
     return (1.0 / 3.0) * start + (2.0 / 3.0) * (here + inc)
 
 
-def lane_gather(tile, index):
-    return jnp.take_along_axis(tile, index, axis=1, mode="promise_in_bounds")
+def split(value):
+    high = value.astype(jnp.bfloat16).astype(jnp.float32)
+    return high, value - high
 
 
 def kernel(
     n_gx, n_gy, cells_all, obs_all,
-    vec_ref, bg_ref, site_ref, off_ref, err_ref,
-    out_ref, obs_ref,
+    vec_hbm, bg_hbm, site_hbm, off_hbm, err_hbm,
+    out_hbm, obs_hbm,
+    out_ref, obs_ref, store_sem,
+    vec_ref, bg_ref, site_ref, off_ref, err_ref, load_sem,
+    weights, lhs, seams, keys, row_w,
     state, one, two, bred, bgrows, strips, edges, proj, gacc, sum_y, sum_x, part,
     send_sem, recv_sem, ysend, yrecv, xsend, xrecv,
 ):
-    groups = site_ref.shape[0]
+    groups = proj.shape[0]
     gx = lax.axis_index("gx")
     gy = lax.axis_index("gy")
     up, dn = lax.rem(gx + n_gx - 1, n_gx), lax.rem(gx + 1, n_gx)
@@ -63,12 +69,24 @@
     sub = lax.broadcasted_iota(jnp.int32, (K, COLS), 0)
     lane8 = lane & 7
 
+    loads = [
+        pltpu.make_async_copy(src, dst, load_sem.at[i])
+        for i, (src, dst) in enumerate(
+            [(bg_hbm, bg_ref), (vec_hbm, vec_ref), (site_hbm, site_ref),
+             (off_hbm, off_ref), (err_hbm, err_ref)]
+        )
+    ]
+    for copy in loads:
+        copy.start()
+
     barrier = pltpu.get_barrier_semaphore()
     greeted = [(a, b) for a in (up, dn) for b in (lf, rt)]
     greeted += [(a, gy) for a in x_peers] + [(gx, b) for b in y_peers]
     for peer in greeted:
         pl.semaphore_signal(barrier, inc=1, device_id=peer, device_id_type=MESH)
 
+    loads[0].wait()
+    loads[1].wait()
     packed = [[jnp.zeros((K, COLS), jnp.float32) for _ in range(V + 1)] for _ in range(2)]
     for l in range(L):
         for r in range(ROWS):
@@ -128,6 +146,40 @@
 
     gacc[...] = jnp.zeros_like(gacc)
     proj[...] = jnp.zeros_like(proj)
+    for copy in loads[2:]:
+        copy.wait()
+
+    cell = lax.broadcasted_iota(jnp.int32, (COLS, COLS), 0)
+    slot = lax.broadcasted_iota(jnp.int32, (16, COLS), 0)
+    weights[pl.ds(3 * COLS, COLS), :] = jnp.zeros((COLS, groups * COLS), jnp.bfloat16)
+
+    def weigh_columns(g, carry):
+        columns = pl.ds(pl.multiple_of(g * COLS, COLS), COLS)
+        site = site_ref[pl.ds(g, 1), :]
+        a, b = off_ref[0:1, columns], off_ref[1:2, columns]
+        row, col = (site >> 7) & 7, site & 127
+        abs_a, abs_b = jnp.abs(a), jnp.abs(b)
+        row0 = jnp.where(a < 0.0, row - 1, row)
+        col0 = jnp.where(b < 0.0, col - 1, col)
+        keys[g] = jnp.broadcast_to((site >> 10) * 16 + row0 + 1, (K, COLS))
+        row_w[g, 0] = jnp.broadcast_to(jnp.where(a < 0.0, abs_a, 1.0 - abs_a), (K, COLS))
+        row_w[g, 1] = jnp.broadcast_to(jnp.where(a < 0.0, 1.0 - abs_a, abs_a), (K, COLS))
+        w0 = jnp.where(b < 0.0, abs_b, 1.0 - abs_b)
+        w1 = jnp.where(b < 0.0, 1.0 - abs_b, abs_b)
+        high, low = split(
+            jnp.where(cell == col0, w0, 0.0) + jnp.where(cell == col0 + 1, w1, 0.0)
+        )
+        weights[pl.ds(0, COLS), columns] = high.astype(jnp.bfloat16)
+        weights[pl.ds(COLS, COLS), columns] = high.astype(jnp.bfloat16)
+        weights[pl.ds(2 * COLS, COLS), columns] = low.astype(jnp.bfloat16)
+        at_left = jnp.where(col0 < 0, w0, 0.0)
+        at_right = jnp.where(col0 >= COLS - 1, w1, 0.0)
+        high, low = split(jnp.where((slot & 1) == 0, at_right, at_left))
+        seam = jnp.where(slot < 4, high, jnp.where(slot < 6, low, 0.0))
+        weights[pl.ds(3 * COLS, 16), columns] = seam.astype(jnp.bfloat16)
+        return carry
+
+    lax.fori_loop(0, groups, weigh_columns, 0)
     for copy in near:
         copy.wait_recv()
 
@@ -212,45 +264,43 @@
         for s in range(SHIFTS):
             gacc[s] = sums[s]
 
-        def group(g, carry):
-            columns = pl.ds(pl.multiple_of(g * COLS, COLS), COLS)
-            site = jnp.broadcast_to(site_ref[pl.ds(g, 1), :], (K, COLS))
-            a = jnp.broadcast_to(off_ref[0:1, columns], (K, COLS))
-            b = jnp.broadcast_to(off_ref[1:2, columns], (K, COLS))
-            plane, row, col = site >> 10, (site >> 7) & 7, site & 127
-            abs_a, abs_b = jnp.abs(a), jnp.abs(b)
-            row0 = jnp.where(a < 0.0, row - 1, row)
-            col0 = jnp.where(b < 0.0, col - 1, col)
-            wr0 = jnp.where(a < 0.0, abs_a, 1.0 - abs_a)
-            wr1 = jnp.where(a < 0.0, 1.0 - abs_a, abs_a)
-            wc0 = jnp.where(b < 0.0, abs_b, 1.0 - abs_b)
-            wc1 = jnp.where(b < 0.0, 1.0 - abs_b, abs_b)
-            past_left, past_right = col0 < 0, col0 >= COLS - 1
-            w_edge = jnp.where(past_left, wc0, jnp.where(past_right, wc1, 0.0))
-            wc0 = jnp.where(past_left, 0.0, wc0)
-            wc1 = jnp.where(past_right, 0.0, wc1)
-            at0, at1 = col0 & (COLS - 1), (col0 + 1) & (COLS - 1)
-            at_edge = (row0 + 4) * 8 + jnp.where(past_left, 4, 3)
-            key = (plane - l) * 16 + row0 + 1
-            zero = jnp.zeros((K, COLS), jnp.float32)
-            low, high, rim = zero, zero, zero
-            for v in range(V):
-                before = None
-                for rr in range(10):
-                    tile = bred[l, v, rr]
-                    value = wc0 * lane_gather(tile, at0) + wc1 * lane_gather(tile, at1)
-                    if before is not None:
-                        high = jnp.where(before, value, high)
-                    if rr < 9:
-                        before = key == v * 64 + rr
-                        low = jnp.where(before, value, low)
-                edge = edges[3, v]
-                value = wr0 * lane_gather(edge, at_edge) + wr1 * lane_gather(edge, at_edge + 8)
-                rim = jnp.where(plane - l == v * 4, w_edge * value, rim)
-            proj[g] += wr0 * low + wr1 * high + rim
+        for v in range(V):
+            high, low = split(edges[3, v])
+            slots = jnp.where(
+                (lane8 == 3) | (lane8 == 4), high,
+                jnp.where((lane8 == 5) | (lane8 == 6), pltpu.roll(low, 2, 1), pltpu.roll(high, 4, 1)),
+            )
+            for rr in range(10):
+                moved = pltpu.roll(slots, COLS - 8 * (rr + 3) - 3, 1)
+                seams[v, rr] = jnp.where(lane < 6, moved, 0.0)
+        high, low = split(bred[l].reshape(M_ROWS, COLS))
+        lhs[:, 0:COLS] = high.astype(jnp.bfloat16)
+        lhs[:, COLS : 2 * COLS] = low.astype(jnp.bfloat16)
+        lhs[:, 2 * COLS : 3 * COLS] = high.astype(jnp.bfloat16)
+        lhs[:, 3 * COLS :] = seams[...].reshape(M_ROWS, COLS).astype(jnp.bfloat16)
+
+        def block(n, carry):
+            columns = pl.ds(pl.multiple_of(n * WIDE, WIDE), WIDE)
+            mixed = jnp.dot(lhs[...], weights[:, columns], preferred_element_type=jnp.float32)
+            for i in range(WIDE // COLS):
+                g = n * (WIDE // COLS) + i
+                key = keys[g] - l * 16
+                low = jnp.zeros((K, COLS), jnp.float32)
+                high = low
+                for v in range(V):
+                    before = None
+                    for rr in range(10):
+                        at = (v * 10 + rr) * K
+                        value = mixed[at : at + K, i * COLS : (i + 1) * COLS]
+                        if before is not None:
+                            high = jnp.where(before, value, high)
+                        if rr < 9:
+                            before = key == v * 64 + rr
+                            low = jnp.where(before, value, low)
+                proj[g] += row_w[g, 0] * low + row_w[g, 1] * high
             return carry
 
-        lax.fori_loop(0, groups, group, 0)
+        lax.fori_loop(0, groups * COLS // WIDE, block, 0)
         return carry
 
     lax.fori_loop(0, L, level, 0)
@@ -316,6 +366,15 @@
             terms = [terms[i] + terms[i + 1] for i in range(0, len(terms), 2)]
         return terms[0]
 
+    def write_obs(g, carry):
+        columns = pl.ds(pl.multiple_of(g * COLS, COLS), COLS)
+        obs_ref[:, columns] = mix(proj[g]) / jnp.sqrt(err_ref[0:1, columns])
+        return carry
+
+    lax.fori_loop(0, groups, write_obs, 0)
+    obs_out = pltpu.make_async_copy(obs_ref, obs_hbm, store_sem.at[0])
+    obs_out.start()
+
     def write(l, carry):
         for v in range(V):
             for r in range(ROWS):
@@ -324,17 +383,15 @@
 
     lax.fori_loop(0, L, write, 0)
 
-    def write_obs(g, carry):
-        columns = pl.ds(pl.multiple_of(g * COLS, COLS), COLS)
-        obs_ref[:, columns] = mix(proj[g]) / jnp.sqrt(err_ref[0:1, columns])
-        return carry
-
-    lax.fori_loop(0, groups, write_obs, 0)
+    out = pltpu.make_async_copy(out_ref, out_hbm, store_sem.at[1])
+    out.start()
     for copy in near:
         copy.wait_send()
     for l in range(L):
         for copy in level_copies(l):
             copy.wait_send()
+    obs_out.wait()
+    out.wait()
 
 
 def local(n_gx, n_gy, vectors, background, obs_site, obs_offset, obs_error):
@@ -345,16 +402,30 @@
         kernel, n_gx, n_gy, float(PLANES * ROWS * COLS * devices), float(obs_dev * devices)
     )
     f32 = jnp.float32
-    vmem = pl.BlockSpec(memory_space=pltpu.VMEM)
+    hbm = pl.BlockSpec(memory_space=pltpu.HBM)
     analysis, obs = pl.pallas_call(
         body,
         out_shape=(
             jax.ShapeDtypeStruct((K * STRIDE, COLS), f32),
             jax.ShapeDtypeStruct((K, obs_dev), f32),
         ),
-        in_specs=[vmem] * 5,
-        out_specs=(vmem, vmem),
+        in_specs=[hbm] * 5,
+        out_specs=(hbm, hbm),
         scratch_shapes=[
+            pltpu.VMEM((K * STRIDE, COLS), f32),
+            pltpu.VMEM((K, obs_dev), f32),
+            pltpu.SemaphoreType.DMA((2,)),
+            pltpu.VMEM((K * STRIDE, COLS), f32),
+            pltpu.VMEM((V * L * ROWS, COLS), f32),
+            pltpu.VMEM((groups, COLS), jnp.int32),
+            pltpu.VMEM((2, obs_dev), f32),
+            pltpu.VMEM((1, obs_dev), f32),
+            pltpu.SemaphoreType.DMA((5,)),
+            pltpu.VMEM((4 * COLS, obs_dev), jnp.bfloat16),
+            pltpu.VMEM((M_ROWS, 4 * COLS), jnp.bfloat16),
+            pltpu.VMEM((V, 10, K, COLS), f32),
+            pltpu.VMEM((groups, K, COLS), jnp.int32),
+            pltpu.VMEM((groups, 2, K, COLS), f32),
             pltpu.VMEM((L, V, 16, K, COLS), f32),
             pltpu.VMEM((V, 16, K, COLS), f32),
             pltpu.VMEM((V, 16, K, COLS), f32),
@@ -375,7 +446,7 @@
             pltpu.SemaphoreType.DMA((n_gx - 1,)),
         ],
         compiler_params=pltpu.CompilerParams(
-            collective_id=0, has_side_effects=True, vmem_limit_bytes=24 * 1024 * 1024
+            collective_id=0, has_side_effects=True, vmem_limit_bytes=63 * 1024 * 1024
         ),
     )(
         vectors.reshape(K * STRIDE, COLS),

time: 63.1 us -> 42.9 us (0.68)
  Pallas kernels: 56.6 us -> 39.6 us
  local copies, waits for them, and re-layouts: 5.38 us -> 2.46 us
    pallas_call x1, Pallas kernels: 56.6 us -> 39.6 us  [local(): pl.pallas_call(body, out_shape=(jax.ShapeDtypeStruct((K * STRIDE, COLS),...]
    unnamed x12 -> x4, local copies, waits for them, and re-layouts: 5.38 us -> 2.46 us
where the time goes in v2:
time: 42.9 us; the launch traced here: 42.7 us
  Pallas kernels  39.6 us (92%)
  local copies, waits for them, and re-layouts  2.46 us (6%)
  between operations  0.65 us (2%)
    pallas_call x1, Pallas kernels, local(): pl.pallas_call(body, out_shape=(jax.ShapeDtypeStruct((K * STRIDE, COLS),...  39.6 us
    unnamed x4, local copies, waits for them, and re-layouts  2.46 us

profile of v2, /device:TPU:0, one launch (start us, length us, event | category | flops | bytes accessed | tf_op | source)
XLA Modules:
  0.0 42.7 jit_solution(16597025150244261464)
XLA Ops:
  0.6 39.6 %shard_map.68 = (f32[768,128]{1,0:T(8,128)}, f32[8,4096]{1,0:T(8,128)}) custom-call(f32[768,128]{1,0:T(8,128)} %bitcast.6, f32[96,128]{1,0:T(8,128)} %bitcast.7, s32[32,128]{1,0:T(8,128)} %bitcast.8, f32[2,4096]{1,0:T(2,128)} %off_hbm.1, f32[1,4096]{1,0:T(1,128)} %bitcast.9), custom_call_target="tpu_custom_call" | custom-call | tf_op jit(solution)/shard_map/pallas_call | solution.py:406
  40.3 0.0 copy-start
  40.3 1.8 %copy.9 = f32[8,3,4,8,128]{4,3,2,1,0:T(8,128)} copy(f32[8,3,4,8,128]{4,3,2,1,0:T(8,128)} %bitcast.5) | data formatting | bytes 786432
  42.1 0.0 copy-done
  42.1 0.7 %copy.10 = f32[8,4096]{1,0:T(8,128)} copy(f32[8,4096]{1,0:T(8,128)S(1)} %copy-done) | data formatting | bytes 262144
Async XLA Ops:
  40.3 1.8 %copy-start = (f32[8,4096]{1,0:T(8,128)S(1)}, f32[8,4096]{1,0:T(8,128)}, u32[]{:S(2)}) copy-start(f32[8,4096]{1,0:T(8,128)} %get-tuple-element.9) | copy-start | bytes 393220

commit v3 on v2

--- a/solution.py
+++ b/solution.py
@@ -19,7 +19,7 @@
 SHIFTS = 5
 N_EDGE = 8
 M_ROWS = V * 10 * K
-WIDE = 512
+WIDE = 256
 N_COPIES = N_EDGE + 2 + 2 * L
 
 
@@ -183,14 +183,14 @@
     for copy in near:
         copy.wait_recv()
 
-    def level(l, carry):
+    for l in range(L):
         whole = []
         for side in range(3):
             fields = []
             for v in range(V + 1):
                 tile = jnp.zeros((K, COLS), jnp.float32)
                 for seg in range(4):
-                    moved = pltpu.roll(strips[side, seg, v], lax.rem((seg + 4 - l) * 32, COLS), 1)
+                    moved = pltpu.roll(strips[side, seg, v], (seg + 4 - l) * 32 % COLS, 1)
                     tile = jnp.where((lane >> 5) == seg, moved, tile)
                 fields.append(tile)
             whole.append(fields)
@@ -215,10 +215,11 @@
         for stage in range(4):
             for v in range(V):
                 left, right = sides[0][stage][v], sides[1][stage][v]
-                edges[stage, v] = jnp.where(
+                edges[l, stage, v] = jnp.where(
                     lane8 == 4, pltpu.roll(left, 1, 1), pltpu.roll(right, COLS - 1, 1)
                 )
 
+    def level(l, carry):
         for copy in level_copies(l):
             copy.wait_recv()
 
@@ -228,7 +229,7 @@
             return (one, two)[stage - 1][v, q]
 
         for stage in range(3):
-            edge = [edges[stage, v] for v in range(V)]
+            edge = [edges[l, stage, v] for v in range(V)]
             for q in range(1 + stage, 15 - stage):
                 bg = [
                     jnp.broadcast_to(bgrows[q // 4, l, pl.ds(v * 4 + q % 4, 1), :], (K, COLS))
@@ -265,7 +266,7 @@
             gacc[s] = sums[s]
 
         for v in range(V):
-            high, low = split(edges[3, v])
+            high, low = split(edges[l, 3, v])
             slots = jnp.where(
                 (lane8 == 3) | (lane8 == 4), high,
                 jnp.where((lane8 == 5) | (lane8 == 6), pltpu.roll(low, 2, 1), pltpu.roll(high, 4, 1)),
@@ -300,7 +301,7 @@
                 proj[g] += row_w[g, 0] * low + row_w[g, 1] * high
             return carry
 
-        lax.fori_loop(0, groups * COLS // WIDE, block, 0)
+        lax.fori_loop(0, groups * COLS // WIDE, block, 0, unroll=8)
         return carry
 
     lax.fori_loop(0, L, level, 0)
@@ -315,7 +316,7 @@
         )
 
     zero = jnp.zeros((K, COLS), jnp.float32)
-    normal = lax.fori_loop(0, groups, weigh, (zero,) * SHIFTS)
+    normal = lax.fori_loop(0, groups, weigh, (zero,) * SHIFTS, unroll=8)
     mine = zero
     for s in range(SHIFTS):
         total = gacc[s] * (1.0 / cells_all) + normal[s] * (1.0 / obs_all)
@@ -371,7 +372,7 @@
         obs_ref[:, columns] = mix(proj[g]) / jnp.sqrt(err_ref[0:1, columns])
         return carry
 
-    lax.fori_loop(0, groups, write_obs, 0)
+    lax.fori_loop(0, groups, write_obs, 0, unroll=4)
     obs_out = pltpu.make_async_copy(obs_ref, obs_hbm, store_sem.at[0])
     obs_out.start()
 
@@ -432,7 +433,7 @@
             pltpu.VMEM((L, V, 10, K, COLS), f32),
             pltpu.VMEM((4, L, 16, COLS), f32),
             pltpu.VMEM((3, 4, V + 1, K, COLS), f32),
-            pltpu.VMEM((4, V, K, COLS), f32),
+            pltpu.VMEM((L, 4, V, K, COLS), f32),
             pltpu.VMEM((groups, K, COLS), f32),
             pltpu.VMEM((SHIFTS, K, COLS), f32),
             pltpu.VMEM((n_gy, K, COLS), f32),

time: 42.9 us -> 36.9 us (0.86)
  Pallas kernels: 39.6 us -> 33.7 us
    pallas_call x1, Pallas kernels: 39.6 us -> 33.7 us  [local(): pl.pallas_call(body, out_shape=(jax.ShapeDtypeStruct((K * STRIDE, COLS),...]
where the time goes in v3:
time: 36.9 us; the launch traced here: 36.8 us
  Pallas kernels  33.7 us (91%)
  local copies, waits for them, and re-layouts  2.46 us (7%)
  between operations  0.65 us (2%)
    pallas_call x1, Pallas kernels, local(): pl.pallas_call(body, out_shape=(jax.ShapeDtypeStruct((K * STRIDE, COLS),...  33.7 us
    unnamed x4, local copies, waits for them, and re-layouts  2.46 us

profile of v3, /device:TPU:0, one launch (start us, length us, event | category | flops | bytes accessed | tf_op | source)
XLA Modules:
  0.0 36.8 jit_solution(785642688627745429)
XLA Ops:
  0.6 33.7 %shard_map.68 = (f32[768,128]{1,0:T(8,128)}, f32[8,4096]{1,0:T(8,128)}) custom-call(f32[768,128]{1,0:T(8,128)} %bitcast.6, f32[96,128]{1,0:T(8,128)} %bitcast.7, s32[32,128]{1,0:T(8,128)} %bitcast.8, f32[2,4096]{1,0:T(2,128)} %off_hbm.1, f32[1,4096]{1,0:T(1,128)} %bitcast.9), custom_call_target="tpu_custom_call" | custom-call | tf_op jit(solution)/shard_map/pallas_call | solution.py:407
  34.3 0.0 copy-start
  34.3 1.8 %copy.9 = f32[8,3,4,8,128]{4,3,2,1,0:T(8,128)} copy(f32[8,3,4,8,128]{4,3,2,1,0:T(8,128)} %bitcast.5) | data formatting | bytes 786432
  36.1 0.0 copy-done
  36.1 0.7 %copy.10 = f32[8,4096]{1,0:T(8,128)} copy(f32[8,4096]{1,0:T(8,128)S(1)} %copy-done) | data formatting | bytes 262144
Async XLA Ops:
  34.3 1.8 %copy-start = (f32[8,4096]{1,0:T(8,128)S(1)}, f32[8,4096]{1,0:T(8,128)}, u32[]{:S(2)}) copy-start(f32[8,4096]{1,0:T(8,128)} %get-tuple-element.9) | copy-start | bytes 393220

commit v4 on v3

--- a/solution.py
+++ b/solution.py
@@ -51,8 +51,7 @@
 def kernel(
     n_gx, n_gy, cells_all, obs_all,
     vec_hbm, bg_hbm, site_hbm, off_hbm, err_hbm,
-    out_hbm, obs_hbm,
-    out_ref, obs_ref, store_sem,
+    bred_hbm, proj_hbm, matrix_ref, store_sem,
     vec_ref, bg_ref, site_ref, off_ref, err_ref, load_sem,
     weights, lhs, seams, keys, row_w,
     state, one, two, bred, bgrows, strips, edges, proj, gacc, sum_y, sum_x, part,
@@ -81,7 +80,15 @@
 
     barrier = pltpu.get_barrier_semaphore()
     greeted = [(a, b) for a in (up, dn) for b in (lf, rt)]
-    greeted += [(a, gy) for a in x_peers] + [(gx, b) for b in y_peers]
+    direct = sum_x.shape[0] == n_gx * n_gy
+    if direct:
+        peers = [
+            (lax.rem(gx + i, n_gx), lax.rem(gy + j, n_gy))
+            for i in range(n_gx) for j in range(n_gy) if i + j > 0
+        ]
+        greeted = peers
+    else:
+        greeted += [(a, gy) for a in x_peers] + [(gx, b) for b in y_peers]
     for peer in greeted:
         pl.semaphore_signal(barrier, inc=1, device_id=peer, device_id_type=MESH)
 
@@ -219,6 +226,11 @@
                     lane8 == 4, pltpu.roll(left, 1, 1), pltpu.roll(right, COLS - 1, 1)
                 )
 
+    def stored(l):
+        return pltpu.make_async_copy(
+            bred.at[l, :, pl.ds(1, ROWS)], bred_hbm.at[l], store_sem.at[l]
+        )
+
     def level(l, carry):
         for copy in level_copies(l):
             copy.wait_recv()
@@ -301,10 +313,13 @@
                 proj[g] += row_w[g, 0] * low + row_w[g, 1] * high
             return carry
 
+        stored(l).start()
         lax.fori_loop(0, groups * COLS // WIDE, block, 0, unroll=8)
         return carry
 
     lax.fori_loop(0, L, level, 0)
+    proj_out = pltpu.make_async_copy(proj, proj_hbm, store_sem.at[L])
+    proj_out.start()
 
     def weigh(g, sums):
         columns = pl.ds(pl.multiple_of(g * COLS, COLS), COLS)
@@ -336,13 +351,16 @@
             copy.start()
         for copy in copies:
             copy.wait()
-        total = slots[0]
-        for i in range(1, len(peers) + 1):
-            total = total + slots[i]
-        return total
-
-    mine = all_sum(mine, sum_y, gy, y_peers, lambda p: (gx, p), ysend, yrecv)
-    mine = all_sum(mine, sum_x, gx, x_peers, lambda p: (p, gy), xsend, xrecv)
+        terms = [slots[i] for i in range(len(peers) + 1)]
+        while len(terms) > 1:
+            terms = [sum(terms[i : i + 2][1:], terms[i]) for i in range(0, len(terms), 2)]
+        return terms[0]
+
+    if direct:
+        mine = all_sum(mine, sum_x, gx * n_gy + gy, peers, lambda p: p, xsend, xrecv)
+    else:
+        mine = all_sum(mine, sum_y, gy, y_peers, lambda p: (gx, p), ysend, yrecv)
+        mine = all_sum(mine, sum_x, gx, x_peers, lambda p: (p, gy), xsend, xrecv)
 
     matrix = jnp.where(lane == sub + K, 1.0, 0.0)
     for s in range(K):
@@ -359,6 +377,33 @@
         scale = jnp.where(sub == j, pivot, scale)
         matrix = jnp.where(sub > j, matrix - (column / pivot) * pivot_row, matrix)
     matrix = matrix / jnp.sqrt(scale)
+    matrix_ref[...] = matrix
+    for copy in near:
+        copy.wait_send()
+    for l in range(L):
+        for copy in level_copies(l):
+            copy.wait_send()
+        stored(l).wait()
+    proj_out.wait()
+
+
+def mix_kernel(
+    bred_hbm, proj_hbm, matrix_hbm, err_hbm, out_hbm, obs_hbm,
+    bred, proj, matrix_ref, err_ref, out, obs, load_sem, out_sem,
+):
+    groups = proj.shape[0]
+    loads = [
+        pltpu.make_async_copy(src, dst, load_sem.at[i])
+        for i, (src, dst) in enumerate([(matrix_hbm, matrix_ref), (err_hbm, err_ref), (proj_hbm, proj)])
+    ]
+    loads += [
+        pltpu.make_async_copy(bred_hbm.at[:, v], bred.at[:, v], load_sem.at[3 + v]) for v in range(V)
+    ]
+    for copy in loads:
+        copy.start()
+    for copy in loads[:3]:
+        copy.wait()
+    matrix = matrix_ref[...]
     combo = [jnp.broadcast_to(matrix[:, K + j : K + j + 1], (K, COLS)) for j in range(K)]
 
     def mix(tile):
@@ -369,30 +414,28 @@
 
     def write_obs(g, carry):
         columns = pl.ds(pl.multiple_of(g * COLS, COLS), COLS)
-        obs_ref[:, columns] = mix(proj[g]) / jnp.sqrt(err_ref[0:1, columns])
+        obs[:, columns] = mix(proj[g]) / jnp.sqrt(err_ref[0:1, columns])
         return carry
 
-    lax.fori_loop(0, groups, write_obs, 0, unroll=4)
-    obs_out = pltpu.make_async_copy(obs_ref, obs_hbm, store_sem.at[0])
-    obs_out.start()
-
-    def write(l, carry):
-        for v in range(V):
+    lax.fori_loop(0, groups, write_obs, 0, unroll=8)
+    stores = [pltpu.make_async_copy(obs, obs_hbm, out_sem.at[0])]
+    stores[0].start()
+    part = L * ROWS
+    for v in range(V):
+        loads[3 + v].wait()
+        for l in range(L):
             for r in range(ROWS):
-                out_ref[pl.ds(v * L * ROWS + l * ROWS + r, K, stride=STRIDE), :] = mix(bred[l, v, r + 1])
-        return carry
-
-    lax.fori_loop(0, L, write, 0)
-
-    out = pltpu.make_async_copy(out_ref, out_hbm, store_sem.at[1])
-    out.start()
-    for copy in near:
-        copy.wait_send()
-    for l in range(L):
-        for copy in level_copies(l):
-            copy.wait_send()
-    obs_out.wait()
-    out.wait()
+                out[pl.ds(v * K * part + l * ROWS + r, K, stride=part), :] = mix(bred[l, v, r])
+        for k in range(K):
+            copy = pltpu.make_async_copy(
+                out.at[pl.ds((v * K + k) * part, part)],
+                out_hbm.at[pl.ds((k * V + v) * part, part)],
+                out_sem.at[1 + v * K + k],
+            )
+            copy.start()
+            stores.append(copy)
+    for copy in stores:
+        copy.wait()
 
 
 def local(n_gx, n_gy, vectors, background, obs_site, obs_offset, obs_error):
@@ -403,19 +446,21 @@
         kernel, n_gx, n_gy, float(PLANES * ROWS * COLS * devices), float(obs_dev * devices)
     )
     f32 = jnp.float32
+    slots = devices if devices <= 64 else n_gx
+    vmem = pl.BlockSpec(memory_space=pltpu.VMEM)
     hbm = pl.BlockSpec(memory_space=pltpu.HBM)
-    analysis, obs = pl.pallas_call(
+    error = obs_error.reshape(1, obs_dev)
+    bred, proj, matrix = pl.pallas_call(
         body,
         out_shape=(
-            jax.ShapeDtypeStruct((K * STRIDE, COLS), f32),
-            jax.ShapeDtypeStruct((K, obs_dev), f32),
+            jax.ShapeDtypeStruct((L, V, ROWS, K, COLS), f32),
+            jax.ShapeDtypeStruct((groups, K, COLS), f32),
+            jax.ShapeDtypeStruct((K, COLS), f32),
         ),
         in_specs=[hbm] * 5,
-        out_specs=(hbm, hbm),
+        out_specs=(hbm, hbm, vmem),
         scratch_shapes=[
-            pltpu.VMEM((K * STRIDE, COLS), f32),
-            pltpu.VMEM((K, obs_dev), f32),
-            pltpu.SemaphoreType.DMA((2,)),
+            pltpu.SemaphoreType.DMA((L + 1,)),
             pltpu.VMEM((K * STRIDE, COLS), f32),
             pltpu.VMEM((V * L * ROWS, COLS), f32),
             pltpu.VMEM((groups, COLS), jnp.int32),
@@ -437,14 +482,14 @@
             pltpu.VMEM((groups, K, COLS), f32),
             pltpu.VMEM((SHIFTS, K, COLS), f32),
             pltpu.VMEM((n_gy, K, COLS), f32),
-            pltpu.VMEM((n_gx, K, COLS), f32),
+            pltpu.VMEM((slots, K, COLS), f32),
             pltpu.VMEM((K, COLS), f32),
             pltpu.SemaphoreType.DMA((N_COPIES,)),
             pltpu.SemaphoreType.DMA((N_COPIES,)),
             pltpu.SemaphoreType.DMA((n_gy - 1,)),
             pltpu.SemaphoreType.DMA((n_gy - 1,)),
-            pltpu.SemaphoreType.DMA((n_gx - 1,)),
-            pltpu.SemaphoreType.DMA((n_gx - 1,)),
+            pltpu.SemaphoreType.DMA((slots - 1,)),
+            pltpu.SemaphoreType.DMA((slots - 1,)),
         ],
         compiler_params=pltpu.CompilerParams(
             collective_id=0, has_side_effects=True, vmem_limit_bytes=63 * 1024 * 1024
@@ -454,8 +499,28 @@
         background.reshape(V * L * ROWS, COLS),
         obs_site.reshape(groups, COLS),
         obs_offset,
-        obs_error.reshape(1, obs_dev),
+        error,
     )
+    analysis, obs = pl.pallas_call(
+        mix_kernel,
+        out_shape=(
+            jax.ShapeDtypeStruct((K * STRIDE, COLS), f32),
+            jax.ShapeDtypeStruct((K, obs_dev), f32),
+        ),
+        in_specs=[hbm] * 4,
+        out_specs=(hbm, hbm),
+        scratch_shapes=[
+            pltpu.VMEM((L, V, ROWS, K, COLS), f32),
+            pltpu.VMEM((groups, K, COLS), f32),
+            pltpu.VMEM((K, COLS), f32),
+            pltpu.VMEM((1, obs_dev), f32),
+            pltpu.VMEM((K * STRIDE, COLS), f32),
+            pltpu.VMEM((K, obs_dev), f32),
+            pltpu.SemaphoreType.DMA((3 + V,)),
+            pltpu.SemaphoreType.DMA((1 + V * K,)),
+        ],
+        compiler_params=pltpu.CompilerParams(vmem_limit_bytes=63 * 1024 * 1024),
+    )(bred, proj, matrix, error)
     return analysis.reshape(vectors.shape), obs
 
 

time: 36.9 us -> 35 us (0.949)
  local copies, waits for them, and re-layouts: 2.46 us -> 0 us
  Pallas kernels: 33.7 us -> 34.2 us
    unnamed x4 -> x0, local copies, waits for them, and re-layouts: 2.46 us -> none
    pallas_call x1 -> x2, Pallas kernels: 33.7 us -> 34.2 us  [the longest x1 31.8 us: local(): pl.pallas_call(body, out_shape=(jax.ShapeDtypeStruct((L, V, ROWS, K, COLS...]
where the time goes in v4:
time: 35 us; the launch traced here: 34.9 us
  Pallas kernels  34.2 us (98%)
  between operations  0.64 us (2%)
    pallas_call x1, Pallas kernels, local(): pl.pallas_call(body, out_shape=(jax.ShapeDtypeStruct((L, V, ROWS, K, COLS...  31.8 us
    pallas_call x1, Pallas kernels, local(): pl.pallas_call(mix_kernel, out_shape=(jax.ShapeDtypeStruct((K * STRIDE, C...  2.44 us

profile of v4, /device:TPU:0, one launch (start us, length us, event | category | flops | bytes accessed | tf_op | source)
XLA Modules:
  0.0 34.9 jit_solution(15256456924252516454)
XLA Ops:
  0.6 31.8 %shard_map.68 = (f32[4,3,8,8,128]{4,3,2,1,0:T(8,128)}, f32[32,8,128]{2,1,0:T(8,128)}, f32[8,128]{1,0:T(8,128)}) custom-call(f32[768,128]{1,0:T(8,128)} %bitcast.5, f32[96,128]{1,0:T(8,128)} %bitcast.8, s32[32,128]{1,0:T(8,128)} %bitcast.9, f32[2,4096]{1,0:T(2,128)} %off_hbm.1, f32[1,4096]{1,0:T(1,128)} %bitcast.6), custom_call_target="tpu_custom_call" | custom-call | tf_op jit(solution)/shard_map/pallas_call | solution.py:453
  32.4 2.4 %shard_map.69 = (f32[768,128]{1,0:T(8,128)}, f32[8,4096]{1,0:T(8,128)}) custom-call(f32[4,3,8,8,128]{4,3,2,1,0:T(8,128)} %get-tuple-element.7.bred_hbm, f32[32,8,128]{2,1,0:T(8,128)} %get-tuple-element.8.proj_hbm, f32[8,128]{1,0:T(8,128)} %get-tuple-element.9.matrix_hbm, f32[1,4096]{1,0:T(1,128)} %bitcast.7), custom_call_target="tpu_custom_call" | custom-call | tf_op jit(solution)/shard_map/pallas_call | solution.py:504

commit v5 on v4

--- a/solution.py
+++ b/solution.py
@@ -20,6 +20,7 @@
 N_EDGE = 8
 M_ROWS = V * 10 * K
 WIDE = 256
+PAIR = 2
 N_COPIES = N_EDGE + 2 + 2 * L
 
 
@@ -231,7 +232,8 @@
             bred.at[l, :, pl.ds(1, ROWS)], bred_hbm.at[l], store_sem.at[l]
         )
 
-    def level(l, carry):
+    def level(i, pair):
+        l = PAIR * pair + i
         for copy in level_copies(l):
             copy.wait_recv()
 
@@ -287,37 +289,43 @@
                 moved = pltpu.roll(slots, COLS - 8 * (rr + 3) - 3, 1)
                 seams[v, rr] = jnp.where(lane < 6, moved, 0.0)
         high, low = split(bred[l].reshape(M_ROWS, COLS))
-        lhs[:, 0:COLS] = high.astype(jnp.bfloat16)
-        lhs[:, COLS : 2 * COLS] = low.astype(jnp.bfloat16)
-        lhs[:, 2 * COLS : 3 * COLS] = high.astype(jnp.bfloat16)
-        lhs[:, 3 * COLS :] = seams[...].reshape(M_ROWS, COLS).astype(jnp.bfloat16)
+        rows = pl.ds(pl.multiple_of(i * M_ROWS, 16), M_ROWS)
+        lhs[rows, 0:COLS] = high.astype(jnp.bfloat16)
+        lhs[rows, COLS : 2 * COLS] = low.astype(jnp.bfloat16)
+        lhs[rows, 2 * COLS : 3 * COLS] = high.astype(jnp.bfloat16)
+        lhs[rows, 3 * COLS :] = seams[...].reshape(M_ROWS, COLS).astype(jnp.bfloat16)
+        stored(l).start()
+        return pair
+
+    def level_pair(pair, carry):
+        lax.fori_loop(0, PAIR, level, pair)
 
         def block(n, carry):
             columns = pl.ds(pl.multiple_of(n * WIDE, WIDE), WIDE)
             mixed = jnp.dot(lhs[...], weights[:, columns], preferred_element_type=jnp.float32)
             for i in range(WIDE // COLS):
                 g = n * (WIDE // COLS) + i
-                key = keys[g] - l * 16
+                key = keys[g] - pair * (PAIR * 16)
                 low = jnp.zeros((K, COLS), jnp.float32)
                 high = low
-                for v in range(V):
-                    before = None
-                    for rr in range(10):
-                        at = (v * 10 + rr) * K
-                        value = mixed[at : at + K, i * COLS : (i + 1) * COLS]
-                        if before is not None:
-                            high = jnp.where(before, value, high)
-                        if rr < 9:
-                            before = key == v * 64 + rr
-                            low = jnp.where(before, value, low)
+                for at_level in range(PAIR):
+                    for v in range(V):
+                        before = None
+                        for rr in range(10):
+                            at = ((at_level * V + v) * 10 + rr) * K
+                            value = mixed[at : at + K, i * COLS : (i + 1) * COLS]
+                            if before is not None:
+                                high = jnp.where(before, value, high)
+                            if rr < 9:
+                                before = key == v * 64 + at_level * 16 + rr
+                                low = jnp.where(before, value, low)
                 proj[g] += row_w[g, 0] * low + row_w[g, 1] * high
             return carry
 
-        stored(l).start()
         lax.fori_loop(0, groups * COLS // WIDE, block, 0, unroll=8)
         return carry
 
-    lax.fori_loop(0, L, level, 0)
+    lax.fori_loop(0, L // PAIR, level_pair, 0)
     proj_out = pltpu.make_async_copy(proj, proj_hbm, store_sem.at[L])
     proj_out.start()
 
@@ -468,7 +476,7 @@
             pltpu.VMEM((1, obs_dev), f32),
             pltpu.SemaphoreType.DMA((5,)),
             pltpu.VMEM((4 * COLS, obs_dev), jnp.bfloat16),
-            pltpu.VMEM((M_ROWS, 4 * COLS), jnp.bfloat16),
+            pltpu.VMEM((PAIR * M_ROWS, 4 * COLS), jnp.bfloat16),
             pltpu.VMEM((V, 10, K, COLS), f32),
             pltpu.VMEM((groups, K, COLS), jnp.int32),
             pltpu.VMEM((groups, 2, K, COLS), f32),

time: 35 us -> 34.7 us (level)
  Pallas kernels: 34.2 us -> 33.8 us
    pallas_call x1, Pallas kernels: 31.8 us -> 31.4 us  [local(): pl.pallas_call(body, out_shape=(jax.ShapeDtypeStruct((L, V, ROWS, K, COLS...]
where the time goes in v5:
time: 34.7 us; the launch traced here: 34.5 us
  Pallas kernels  33.8 us (97%)
  between operations  0.64 us (2%)
    pallas_call x1, Pallas kernels, local(): pl.pallas_call(body, out_shape=(jax.ShapeDtypeStruct((L, V, ROWS, K, COLS...  31.4 us
    pallas_call x1, Pallas kernels, local(): pl.pallas_call(mix_kernel, out_shape=(jax.ShapeDtypeStruct((K * STRIDE, C...  2.44 us

profile of v5, /device:TPU:0, one launch (start us, length us, event | category | flops | bytes accessed | tf_op | source)
XLA Modules:
  0.0 34.5 jit_solution(13941669385116394664)
XLA Ops:
  0.6 31.4 %shard_map.68 = (f32[4,3,8,8,128]{4,3,2,1,0:T(8,128)}, f32[32,8,128]{2,1,0:T(8,128)}, f32[8,128]{1,0:T(8,128)}) custom-call(f32[768,128]{1,0:T(8,128)} %bitcast.5, f32[96,128]{1,0:T(8,128)} %bitcast.8, s32[32,128]{1,0:T(8,128)} %bitcast.9, f32[2,4096]{1,0:T(2,128)} %off_hbm.1, f32[1,4096]{1,0:T(1,128)} %bitcast.6), custom_call_target="tpu_custom_call" | custom-call | tf_op jit(solution)/shard_map/pallas_call | solution.py:461
  32.0 2.4 %shard_map.69 = (f32[768,128]{1,0:T(8,128)}, f32[8,4096]{1,0:T(8,128)}) custom-call(f32[4,3,8,8,128]{4,3,2,1,0:T(8,128)} %get-tuple-element.7.bred_hbm, f32[32,8,128]{2,1,0:T(8,128)} %get-tuple-element.8.proj_hbm, f32[8,128]{1,0:T(8,128)} %get-tuple-element.9.matrix_hbm, f32[1,4096]{1,0:T(1,128)} %bitcast.7), custom_call_target="tpu_custom_call" | custom-call | tf_op jit(solution)/shard_map/pallas_call | solution.py:512

commit v6 on v5

--- a/solution.py
+++ b/solution.py
@@ -148,7 +148,7 @@
 
     for copy in near:
         copy.start()
-    for l in range(L):
+    for l in range(PAIR):
         for copy in level_copies(l):
             copy.start()
 
@@ -188,6 +188,12 @@
         return carry
 
     lax.fori_loop(0, groups, weigh_columns, 0)
+    for l in range(PAIR):
+        for copy in level_copies(l):
+            copy.wait_send()
+    for l in range(PAIR, L):
+        for copy in level_copies(l):
+            copy.start()
     for copy in near:
         copy.wait_recv()
 
@@ -389,8 +395,9 @@
     for copy in near:
         copy.wait_send()
     for l in range(L):
-        for copy in level_copies(l):
-            copy.wait_send()
+        if l >= PAIR:
+            for copy in level_copies(l):
+                copy.wait_send()
         stored(l).wait()
     proj_out.wait()
 

time: 34.7 us -> 33.6 us (0.968)
  Pallas kernels: 33.8 us -> 32.8 us
    pallas_call x1, Pallas kernels: 31.4 us -> 30.4 us  [local(): pl.pallas_call(body, out_shape=(jax.ShapeDtypeStruct((L, V, ROWS, K, COLS...]
where the time goes in v6:
time: 33.6 us; the launch traced here: 33.5 us
  Pallas kernels  32.8 us (98%)
  between operations  0.64 us (2%)
    pallas_call x1, Pallas kernels, local(): pl.pallas_call(body, out_shape=(jax.ShapeDtypeStruct((L, V, ROWS, K, COLS...  30.4 us
    pallas_call x1, Pallas kernels, local(): pl.pallas_call(mix_kernel, out_shape=(jax.ShapeDtypeStruct((K * STRIDE, C...  2.44 us

profile of v6, /device:TPU:0, one launch (start us, length us, event | category | flops | bytes accessed | tf_op | source)
XLA Modules:
  0.0 33.5 jit_solution(10620168110104253801)
XLA Ops:
  0.6 30.4 %shard_map.68 = (f32[4,3,8,8,128]{4,3,2,1,0:T(8,128)}, f32[32,8,128]{2,1,0:T(8,128)}, f32[8,128]{1,0:T(8,128)}) custom-call(f32[768,128]{1,0:T(8,128)} %bitcast.5, f32[96,128]{1,0:T(8,128)} %bitcast.8, s32[32,128]{1,0:T(8,128)} %bitcast.9, f32[2,4096]{1,0:T(2,128)} %off_hbm.1, f32[1,4096]{1,0:T(1,128)} %bitcast.6), custom_call_target="tpu_custom_call" | custom-call | tf_op jit(solution)/shard_map/pallas_call | solution.py:468
  31.0 2.4 %shard_map.69 = (f32[768,128]{1,0:T(8,128)}, f32[8,4096]{1,0:T(8,128)}) custom-call(f32[4,3,8,8,128]{4,3,2,1,0:T(8,128)} %get-tuple-element.7.bred_hbm, f32[32,8,128]{2,1,0:T(8,128)} %get-tuple-element.8.proj_hbm, f32[8,128]{1,0:T(8,128)} %get-tuple-element.9.matrix_hbm, f32[1,4096]{1,0:T(1,128)} %bitcast.7), custom_call_target="tpu_custom_call" | custom-call | tf_op jit(solution)/shard_map/pallas_call | solution.py:519

commit v7 on v6

--- a/solution.py
+++ b/solution.py
@@ -240,13 +240,11 @@
 
     def level(i, pair):
         l = PAIR * pair + i
-        for copy in level_copies(l):
-            copy.wait_recv()
 
         def read(stage, v, q):
             if stage == 0:
                 return state[l, v, q]
-            return (one, two)[stage - 1][v, q]
+            return (one, two)[stage - 1][i, v, q]
 
         for stage in range(3):
             edge = [edges[l, stage, v] for v in range(V)]
@@ -269,9 +267,9 @@
                 for v in range(V):
                     value = advance(stage, state[l, v, q], here[v], inc[v])
                     if stage == 0:
-                        one[v, q] = value
+                        one[i, v, q] = value
                     elif stage == 1:
-                        two[v, q] = value
+                        two[i, v, q] = value
                     else:
                         bred[l, v, q - 3] = value
 
@@ -293,18 +291,21 @@
             )
             for rr in range(10):
                 moved = pltpu.roll(slots, COLS - 8 * (rr + 3) - 3, 1)
-                seams[v, rr] = jnp.where(lane < 6, moved, 0.0)
+                seams[i, v, rr] = jnp.where(lane < 6, moved, 0.0)
         high, low = split(bred[l].reshape(M_ROWS, COLS))
-        rows = pl.ds(pl.multiple_of(i * M_ROWS, 16), M_ROWS)
+        rows = pl.ds(i * M_ROWS, M_ROWS)
         lhs[rows, 0:COLS] = high.astype(jnp.bfloat16)
         lhs[rows, COLS : 2 * COLS] = low.astype(jnp.bfloat16)
         lhs[rows, 2 * COLS : 3 * COLS] = high.astype(jnp.bfloat16)
-        lhs[rows, 3 * COLS :] = seams[...].reshape(M_ROWS, COLS).astype(jnp.bfloat16)
+        lhs[rows, 3 * COLS :] = seams[i].reshape(M_ROWS, COLS).astype(jnp.bfloat16)
         stored(l).start()
-        return pair
 
     def level_pair(pair, carry):
-        lax.fori_loop(0, PAIR, level, pair)
+        for i in range(PAIR):
+            for copy in level_copies(PAIR * pair + i):
+                copy.wait_recv()
+        for i in range(PAIR):
+            level(i, pair)
 
         def block(n, carry):
             columns = pl.ds(pl.multiple_of(n * WIDE, WIDE), WIDE)
@@ -328,7 +329,7 @@
                 proj[g] += row_w[g, 0] * low + row_w[g, 1] * high
             return carry
 
-        lax.fori_loop(0, groups * COLS // WIDE, block, 0, unroll=8)
+        lax.fori_loop(0, groups * COLS // WIDE, block, 0, unroll=16)
         return carry
 
     lax.fori_loop(0, L // PAIR, level_pair, 0)
@@ -484,12 +485,12 @@
             pltpu.SemaphoreType.DMA((5,)),
             pltpu.VMEM((4 * COLS, obs_dev), jnp.bfloat16),
             pltpu.VMEM((PAIR * M_ROWS, 4 * COLS), jnp.bfloat16),
-            pltpu.VMEM((V, 10, K, COLS), f32),
+            pltpu.VMEM((PAIR, V, 10, K, COLS), f32),
             pltpu.VMEM((groups, K, COLS), jnp.int32),
             pltpu.VMEM((groups, 2, K, COLS), f32),
             pltpu.VMEM((L, V, 16, K, COLS), f32),
-            pltpu.VMEM((V, 16, K, COLS), f32),
-            pltpu.VMEM((V, 16, K, COLS), f32),
+            pltpu.VMEM((PAIR, V, 16, K, COLS), f32),
+            pltpu.VMEM((PAIR, V, 16, K, COLS), f32),
             pltpu.VMEM((L, V, 10, K, COLS), f32),
             pltpu.VMEM((4, L, 16, COLS), f32),
             pltpu.VMEM((3, 4, V + 1, K, COLS), f32),

time: 33.6 us -> 33.8 us (level)
  no operation moved by 1% of the time
where the time goes in v7:
time: 33.8 us; the launch traced here: 33.6 us
  Pallas kernels  33 us (98%)
  between operations  0.64 us (2%)
    pallas_call x1, Pallas kernels, local(): pl.pallas_call(body, out_shape=(jax.ShapeDtypeStruct((L, V, ROWS, K, COLS...  30.5 us
    pallas_call x1, Pallas kernels, local(): pl.pallas_call(mix_kernel, out_shape=(jax.ShapeDtypeStruct((K * STRIDE, C...  2.44 us

profile of v7, /device:TPU:0, one launch (start us, length us, event | category | flops | bytes accessed | tf_op | source)
XLA Modules:
  0.0 33.6 jit_solution(7759677079357676454)
XLA Ops:
  0.6 30.5 %shard_map.68 = (f32[4,3,8,8,128]{4,3,2,1,0:T(8,128)}, f32[32,8,128]{2,1,0:T(8,128)}, f32[8,128]{1,0:T(8,128)}) custom-call(f32[768,128]{1,0:T(8,128)} %bitcast.5, f32[96,128]{1,0:T(8,128)} %bitcast.8, s32[32,128]{1,0:T(8,128)} %bitcast.9, f32[2,4096]{1,0:T(2,128)} %off_hbm.1, f32[1,4096]{1,0:T(1,128)} %bitcast.6), custom_call_target="tpu_custom_call" | custom-call | tf_op jit(solution)/shard_map/pallas_call | solution.py:469
  31.2 2.4 %shard_map.69 = (f32[768,128]{1,0:T(8,128)}, f32[8,4096]{1,0:T(8,128)}) custom-call(f32[4,3,8,8,128]{4,3,2,1,0:T(8,128)} %get-tuple-element.7.bred_hbm, f32[32,8,128]{2,1,0:T(8,128)} %get-tuple-element.8.proj_hbm, f32[8,128]{1,0:T(8,128)} %get-tuple-element.9.matrix_hbm, f32[1,4096]{1,0:T(1,128)} %bitcast.7), custom_call_target="tpu_custom_call" | custom-call | tf_op jit(solution)/shard_map/pallas_call | solution.py:520

commit v8 on v6

--- a/solution.py
+++ b/solution.py
@@ -188,12 +188,6 @@
         return carry
 
     lax.fori_loop(0, groups, weigh_columns, 0)
-    for l in range(PAIR):
-        for copy in level_copies(l):
-            copy.wait_send()
-    for l in range(PAIR, L):
-        for copy in level_copies(l):
-            copy.start()
     for copy in near:
         copy.wait_recv()
 
@@ -232,6 +226,13 @@
                 edges[l, stage, v] = jnp.where(
                     lane8 == 4, pltpu.roll(left, 1, 1), pltpu.roll(right, COLS - 1, 1)
                 )
+
+    for l in range(PAIR):
+        for copy in level_copies(l):
+            copy.wait_send()
+    for l in range(PAIR, L):
+        for copy in level_copies(l):
+            copy.start()
 
     def stored(l):
         return pltpu.make_async_copy(

time: 33.6 us -> 33.7 us (level)
  no operation moved by 1% of the time
where the time goes in v8:
time: 33.7 us; the launch traced here: 33.6 us
  Pallas kernels  32.9 us (98%)
  between operations  0.64 us (2%)
    pallas_call x1, Pallas kernels, local(): pl.pallas_call(body, out_shape=(jax.ShapeDtypeStruct((L, V, ROWS, K, COLS...  30.5 us
    pallas_call x1, Pallas kernels, local(): pl.pallas_call(mix_kernel, out_shape=(jax.ShapeDtypeStruct((K * STRIDE, C...  2.44 us

profile of v8, /device:TPU:0, one launch (start us, length us, event | category | flops | bytes accessed | tf_op | source)
XLA Modules:
  0.0 33.6 jit_solution(1724584075763679609)
XLA Ops:
  0.6 30.5 %shard_map.68 = (f32[4,3,8,8,128]{4,3,2,1,0:T(8,128)}, f32[32,8,128]{2,1,0:T(8,128)}, f32[8,128]{1,0:T(8,128)}) custom-call(f32[768,128]{1,0:T(8,128)} %bitcast.5, f32[96,128]{1,0:T(8,128)} %bitcast.8, s32[32,128]{1,0:T(8,128)} %bitcast.9, f32[2,4096]{1,0:T(2,128)} %off_hbm.1, f32[1,4096]{1,0:T(1,128)} %bitcast.6), custom_call_target="tpu_custom_call" | custom-call | tf_op jit(solution)/shard_map/pallas_call | solution.py:469
  31.1 2.4 %shard_map.69 = (f32[768,128]{1,0:T(8,128)}, f32[8,4096]{1,0:T(8,128)}) custom-call(f32[4,3,8,8,128]{4,3,2,1,0:T(8,128)} %get-tuple-element.7.bred_hbm, f32[32,8,128]{2,1,0:T(8,128)} %get-tuple-element.8.proj_hbm, f32[8,128]{1,0:T(8,128)} %get-tuple-element.9.matrix_hbm, f32[1,4096]{1,0:T(1,128)} %bitcast.7), custom_call_target="tpu_custom_call" | custom-call | tf_op jit(solution)/shard_map/pallas_call | solution.py:520
